TPU v7x, 128 devices: a whole 4x4x4 slice. The times are simulated.
128 devices in a mesh: lon: 16 (over x, z_hi, core), lat: 8 (over z_lo, y).
Axes of the slice: x: 4, y: 4, z: 4 (z_hi: 2, z_lo: 2; z = z_hi * 2 + z_lo), core: 2. Of those that a mesh axis runs over, the one named last changes fastest.
Arguments:
- features: bfloat16 [128, 2048, 256], P('lat', 'lon'), may hold values from -6 to 6
- cotangent: bfloat16 [128, 2048, 256], P('lat', 'lon'), may hold values from -6 to 6
- land_sea: int32 [128, 2048], P('lat', 'lon'), may hold values from 0 to 1, as said below
- tile_slot: int32 [128, 16], P('lat', 'lon'), may hold values from 0 to 64, as said below
- kernel: float32 [7, 7, 256], replicated, may hold values from -0.875 to 0.875
- ln_gain: float32 [256], replicated, may hold values from 0.5 to 1.5
- ln_bias: float32 [256], replicated, may hold values from -3 to 3
- w_in: bfloat16 [256, 1024], replicated, may hold values from -0.375 to 0.375
- b_in: float32 [1024], replicated, may hold values from -3 to 3
- w_out: bfloat16 [1024, 256], replicated, may hold values from -0.1875 to 0.1875
- layer_scale: float32 [256], replicated, may hold values from 0.3 to 1.5
Outputs:
- output: bfloat16 [128, 2048, 256], P('lat', 'lon')
- grad_features: bfloat16 [128, 2048, 256], P('lat', 'lon')
- grad_w_in: float32 [256, 1024], replicated
- grad_w_out: float32 [1024, 256], replicated
- grad_kernel: float32 [7, 7, 256], replicated
- grad_layer_scale: float32 [256], replicated
Inputs may be any that keep to these rules, and one draw needn't show every extreme that they name: `tile_slot`: in each longitude column a value v < 64 names an owner band v // 8 and a slot v % 8 there, distinct within the column; 64 marks a tile without work. Of one device's tiles at most 2 name any one other band, a bound reached in every draw; some owner has all 8 slots taken in every column. `land_sea`: every cell of a tile whose tile_slot is 64 is land.
All inputs are finite; a program needn't handle non-finite values.
Results may differ from a plain program's by a relative error of at most 0.012.
Values may be sent and summed in bfloat16 or wider, within the bound.
No kernel may reach another device: no remote copies, remote signals or barrier semaphores. Data moves between devices by JAX's collectives and lax.ppermute only.
A program may use at most 64 MiB of HBM per device.

v0:
```python
import math

import jax
import jax.numpy as jnp
from jax import lax
from jax.sharding import PartitionSpec as P

KS = 7
SEND = 2


GELU_SCALE = math.sqrt(2.0 / math.pi)
GELU_CUBE = 0.044715
EPSILON = 1e-06


def padded_2(block, sides, width):
    for axis, dim in sides:
        count = lax.axis_size(axis)
        forward = [(i, i + 1) for i in range(count - 1)]
        forward.append((count - 1, 0))
        backward = [(target, source) for source, target in forward]
        low = lax.ppermute(
            lax.slice_in_dim(block, block.shape[dim] - width, None, axis=dim), axis, forward
        )
        high = lax.ppermute(lax.slice_in_dim(block, 0, width, axis=dim), axis, backward)
        block = jnp.concatenate([low, block, high], axis=dim)
    return block


def gelu_parts(hidden):
    inside = GELU_SCALE * (hidden + GELU_CUBE * hidden * hidden * hidden)
    hyper = jnp.tanh(inside)
    activated = 0.5 * hidden * (1.0 + hyper)
    derivative = 0.5 * (1.0 + hyper) + 0.5 * hidden * (1.0 - hyper * hyper) * GELU_SCALE * (
        1.0 + 3.0 * GELU_CUBE * hidden * hidden
    )
    return (activated, derivative)


def pointwise(norm_rows, grad_rows, w_in, b_in, w_out):
    hidden = jnp.dot(norm_rows, w_in, preferred_element_type=jnp.float32) + b_in
    activated, derivative = gelu_parts(hidden)
    act_low = activated.astype(jnp.bfloat16)
    result = jnp.dot(act_low, w_out, preferred_element_type=jnp.float32).astype(jnp.bfloat16)
    grad_act = jnp.dot(grad_rows, w_out.T, preferred_element_type=jnp.float32)
    grad_hidden = (grad_act * derivative).astype(jnp.bfloat16)
    grad_wo = jnp.dot(act_low.T, grad_rows, preferred_element_type=jnp.float32)
    grad_wi = jnp.dot(norm_rows.T, grad_hidden, preferred_element_type=jnp.float32)
    grad_norm = jnp.dot(grad_hidden, w_in.T, preferred_element_type=jnp.float32).astype(
        jnp.bfloat16
    )
    return (result, grad_norm, grad_wi, grad_wo)


def extend_rim(field):
    margin = KS // 2
    rows = field.shape[0]
    padded = padded_2(field, (("lon", 1), ("lat", 0)), margin)
    band = lax.axis_index("lat")
    row_ids = lax.broadcasted_iota(jnp.int32, (rows + 2 * margin, 1, 1), 0)
    top_ok = (row_ids >= margin) | (band > 0)
    bottom_ok = (row_ids < rows + margin) | (band < lax.axis_size("lat") - 1)
    return jnp.where(top_ok & bottom_ok, padded, jnp.zeros_like(padded))


def on_device(
    features,
    cotangent,
    land_sea,
    tile_slot,
    kernel,
    ln_gain,
    ln_bias,
    w_in,
    b_in,
    w_out,
    layer_scale,
):
    rows, tile, width = features.shape
    lat_count = lax.axis_size("lat")
    lon_count = lax.axis_size("lon")
    capacity = rows - SEND * lat_count // 2
    slot_total = capacity * lat_count
    padded = extend_rim(features).astype(jnp.float32)
    mixed = jnp.zeros(features.shape, jnp.float32)
    for row_off in range(KS):
        for col_off in range(KS):
            mixed = (
                mixed
                + kernel[row_off, col_off]
                * padded[row_off : row_off + rows, col_off : col_off + tile]
            )
    row_mean = jnp.mean(mixed, axis=-1, keepdims=True)
    centered = mixed - row_mean
    row_var = jnp.mean(centered * centered, axis=-1, keepdims=True)
    inverse_scale = lax.rsqrt(row_var + EPSILON)
    normed = centered * inverse_scale
    normalized = (normed * ln_gain + ln_bias).astype(jnp.bfloat16)
    listed = (tile_slot < slot_total).astype(jnp.float32)
    weight_mask = listed * land_sea.astype(jnp.float32)
    branch_gate = weight_mask[:, :, None] * layer_scale
    cot_wide = cotangent.astype(jnp.float32)
    grad_out = (branch_gate * cot_wide).astype(jnp.bfloat16)
    branch, grad_norm_home, grad_wi, grad_wo = pointwise(
        normalized.reshape(rows * tile, width),
        grad_out.reshape(rows * tile, width),
        w_in,
        b_in,
        w_out,
    )
    branch_wide = branch.reshape(rows, tile, width).astype(jnp.float32)
    output = (features.astype(jnp.float32) + branch_gate * branch_wide).astype(jnp.bfloat16)
    scale_sum = jnp.sum(weight_mask[:, :, None] * cot_wide * branch_wide, axis=(0, 1))
    grad_normed = grad_norm_home.reshape(rows, tile, width).astype(jnp.float32) * ln_gain
    grad_mixed = (
        inverse_scale
        * (
            grad_normed
            - jnp.mean(grad_normed, axis=-1, keepdims=True)
            - normed * jnp.mean(grad_normed * normed, axis=-1, keepdims=True)
        )
    ).astype(jnp.bfloat16)
    grad_pad = extend_rim(grad_mixed).astype(jnp.float32)
    grad_wide = grad_mixed.astype(jnp.float32)
    grad_features = cot_wide
    kernel_rows = []
    for row_off in range(KS):
        for col_off in range(KS):
            flip_row = KS - 1 - row_off
            flip_col = KS - 1 - col_off
            grad_features = (
                grad_features
                + kernel[row_off, col_off]
                * grad_pad[flip_row : flip_row + rows, flip_col : flip_col + tile]
            )
            kernel_rows.append(
                jnp.sum(
                    grad_wide * padded[row_off : row_off + rows, col_off : col_off + tile],
                    axis=(0, 1),
                )
            )
    kernel_sum = jnp.stack(kernel_rows).reshape(KS, KS, width)
    total_wi, total_wo, total_kernel, total_scale = lax.psum(
        (grad_wi, grad_wo, kernel_sum, scale_sum), ("lon", "lat")
    )
    factor = 1.0 / math.sqrt(rows * lat_count * tile * lon_count)
    return (
        output,
        grad_features.astype(jnp.bfloat16),
        total_wi * factor,
        total_wo * factor,
        total_kernel * factor,
        total_scale * factor,
    )


def solution(mesh):
    return jax.shard_map(
        on_device,
        mesh=mesh,
        in_specs=(
            P("lat", "lon", None),
            P("lat", "lon", None),
            P("lat", "lon"),
            P("lat", "lon"),
            P(),
            P(),
            P(),
            P(),
            P(),
            P(),
            P(),
        ),
        out_specs=(P("lat", "lon", None), P("lat", "lon", None), P(), P(), P(), P()),
        check_vma=False,
    )
```

profile of v0, /device:TPU:0, one launch (start us, length us, event | category | flops | bytes accessed | tf_op | source)
XLA Modules:
  0.0 349.7 jit_solution(1480222451890777438)
XLA Ops:
  7.2 1.0 fusion.115
  8.3 5.7 %collective-permute-start.1 = (bf16[16,3,256]{2,1,0:T(4,128)(2,1)S(1)}, bf16[16,3,256]{2,1,0:T(4,128)(2,1)S(1)}, u32[]{:S(2)}, u32[]{:S(2)}) collective-permute-start(bf16[16,3,256]{2,1,0:T(4,128)(2,1)S(1)} %get-tuple-element.71), channel_id=1, source_target_pairs={{8,0},{16,8},{24,16},{32,24},{40,32},{48,40},{56,48},{64,56},{72,6... | collective-permute-start | bytes 73736 | tf_op jit(solution)/shard_map/ppermute | solution.py:26
  14.0 0.9 fusion.118
  14.9 1.0 fusion.116
  15.9 1.0 fusion.117
  17.6 1.1 pad_maximum_fusion.5
  18.8 1.6 collective-permute-start.2
  20.4 2.6 collective-permute-start.3
  23.8 3.8 %collective-permute-done.2 = bf16[3,134,256]{2,1,0:T(8,128)(2,1)S(1)} collective-permute-done((bf16[3,134,256]{2,1,0:T(8,128)(2,1)S(1)}, bf16[3,134,256]{2,1,0:T(8,128)(2,1)S(1)}, u32[]{:S(2)}, u32[]{:S(2)}) %collective-permute-start.2) | collective-permute-done | bytes 205856 | tf_op jit(solution)/shard_map/ppermute | solution.py:23
  27.6 2.2 fusion.110
  29.8 49.0 %fusion.113 = (f32[16,128]{1,0:T(8,128)S(1)}, f32[16,128,256]{2,1,0:T(8,128)S(1)}) fusion(f32[22,134,256]{2,1,0:T(8,128)} %fusion.110, f32[256]{0:T(256)S(1)} %bitcast.146, f32[256]{0:T(256)S(1)} %bitcast.148, f32[256]{0:T(256)S(1)} %bitcast.152, f32[256]{0:T(256)S(1)} %bitcast.154, f32[256]{0:T(256)S(1)} %bitcast.156, f32[256]{0:T(256)S(1)} %bitcast.158, ...), kind=kLoop, calls=%fused_computation.247 | loop fusion | flops 51378176 | bytes 104915968 | tf_op jit(solution)/shard_map/reduce_sum | solution.py:94
  80.3 3.7 %multiply_convert_fusion = (bf16[2048,1024]{1,0:T(8,128)(2,1)S(1)}, f32[2048,1024]{1,0:T(8,128)S(1)}) fusion(f32[1024]{0:T(1024)S(1)} %copy-done.13, bf16[2048,256]{1,0:T(8,128)(2,1)S(1)} %bitcast.126, bf16[256,1024]{1,0:T(8,128)(2,1)S(1)} %copy-done), kind=kOutput, calls=%fused_computation.58 | convolution fusion | flops 1094713344 | bytes 14159872 | tf_op jit(solution)/shard_map/dot_general | solution.py:42
  84.1 1.3 convolution_convert_fusion.1
  85.6 1.8 fusion.8
  87.4 2.3 fusion.120
  89.7 7.2 %fusion.6 = bf16[2048,1024]{1,0:T(8,128)(2,1)} fusion(f32[2048,1024]{1,0:T(8,128)S(1)} %get-tuple-element.123, bf16[2048,256]{1,0:T(8,128)(2,1)S(1)} %bitcast.125, bf16[1024,256]{1,0:T(8,128)(2,1)S(1)} %copy-done.12, f32[1024]{0:T(1024)S(1)} %copy-done.13), kind=kOutput, calls=%fused_computation.57 | convolution fusion | flops 1115684864 | bytes 14159872 | tf_op jit(solution)/shard_map/dot_general | solution.py:46
  96.9 4.4 %fusion.119 = f32[256,1024]{1,0:T(8,128)} fusion(bf16[2048,256]{1,0:T(8,128)(2,1)S(1)} %bitcast.127, bf16[2048,1024]{1,0:T(8,128)(2,1)} %fusion.6), kind=kOutput, calls=%fused_computation.253 | convolution fusion | flops 1073741824 | bytes 6291456 | tf_op jit(solution)/shard_map/dot_general | solution.py:49
  101.3 3.6 %multiply_reduce_fusion.1 = (f32[2048]{0:T(1024)S(1)}, f32[2048,256]{1,0:T(8,128)S(1)}) fusion(f32[256]{0:T(256)S(1)} %copy-done.9, bf16[2048,1024]{1,0:T(8,128)(2,1)} %fusion.6, bf16[256,1024]{1,0:T(8,128)(2,1)S(1)} %copy-done), kind=kOutput, calls=%fused_computation.220 | convolution fusion | flops 1075836928 | bytes 6824960 | tf_op jit(solution)/shard_map/dot_general | solution.py:50
  104.9 1.0 multiply_reduce_fusion
  106.7 5.6 %fusion.84 = (f32[256]{0:T(256)S(1)}, f32[256]{0:T(256)S(1)}, f32[256]{0:T(256)S(1)}, f32[256]{0:T(256)S(1)}, f32[256]{0:T(256)S(1)}, /*index=5*/f32[256]{0:T(25...) fusion(f32[22,134,256]{2,1,0:T(8,128)S(1)} %copy-done.1, ...), kind=kLoop, calls=%fused_computation.143 | loop fusion | flops 23588352 | bytes 43043840 | tf_op jit(solution)/shard_map/reduce_sum | solution.py:138
  112.3 3.3 fusion.83
  115.7 4.9 %fusion.85 = (f32[256]{0:T(256)S(1)}, f32[256]{0:T(256)S(1)}, f32[256]{0:T(256)S(1)}, f32[256]{0:T(256)S(1)}, f32[256]{0:T(256)S(1)}, /*index=5*/f32[256]{0:T(25...) fusion(bf16[16,128,256]{2,1,0:T(8,128)(2,1)S(1)} %get-tuple-ele, ...), kind=kLoop, calls=%fused_computation.144 | loop fusion | flops 19394048 | bytes 38815744 | tf_op jit(solution)/shard_map/reduce_sum | solution.py:138
  120.9 5.3 %collective-permute-start.5 = (bf16[16,3,256]{2,1,0:T(4,128)(2,1)S(1)}, bf16[16,3,256]{2,1,0:T(4,128)(2,1)S(1)}, u32[]{:S(2)}, u32[]{:S(2)}) collective-permute-start(bf16[16,3,256]{2,1,0:T(4,128)(2,1)S(1)} %get-tuple-element.69), channel_id=1, source_target_pairs={{8,0},{16,8},{24,16},{32,24},{40,32},{48,40},{56,48},{64,56},{72,6... | collective-permute-start | bytes 73736 | tf_op jit(solution)/shard_map/ppermute | solution.py:26
  126.2 64.3 %all-reduce = (f32[7,7,256]{2,1,0:T(8,128)S(1)}, f32[256]{0:T(256)S(1)}) all-reduce(f32[7,7,256]{2,1,0:T(8,128)S(1)} %reshape.75, f32[256]{0:T(256)S(1)} %get-tuple-element.66), channel_id=1, replica_groups=mesh['lon'=16,'lat'=8] {'lon','lat'}, use_global_device_ids=true, to_apply=%region_55.56 | all-reduce | flops 12800 | bytes 102400 | tf_op jit(solution)/shard_map/psum | solution.py:144
  191.3 1.4 collective-permute-start.6
  192.8 2.8 collective-permute-start.7
  196.1 4.4 %collective-permute-done.6 = bf16[3,134,256]{2,1,0:T(8,128)(2,1)S(1)} collective-permute-done((bf16[3,134,256]{2,1,0:T(8,128)(2,1)S(1)}, bf16[3,134,256]{2,1,0:T(8,128)(2,1)S(1)}, u32[]{:S(2)}, u32[]{:S(2)}) %collective-permute-start.6) | collective-permute-done | bytes 205856 | tf_op jit(solution)/shard_map/ppermute | solution.py:23
  200.6 2.2 fusion.111
  202.8 49.9 %fusion.87 = bf16[16,128,256]{2,1,0:T(8,128)(2,1)} fusion(f32[22,134,256]{2,1,0:T(8,128)} %fusion.111, bf16[16,128,256]{2,1,0:T(8,128)(2,1)S(1)} %copy-done.7, f32[256]{0:T(256)S(1)} %bitcast.147, f32[256]{0:T(256)S(1)} %bitcast.149, f32[256]{0:T(256)S(1)} %bitcast.153, f32[256]{0:T(256)S(1)} %bitcast.155, f32[256]{0:T(256)S(1)} %bitcast.157, ...), kind=kLoop, calls=%fused_computation.147 | loop fusion | flops 52428800 | bytes 104907776 | tf_op jit(solution)/shard_map/convert_element_type | solution.py:150
  252.7 86.8 %all-reduce.4.cloned.1.call-done = (f32[256,1024]{1,0:T(8,128)}, f32[1024,256]{1,0:T(8,128)}) async-done(((f32[256,1024]{1,0:T(8,128)}, f32[1024,256]{1,0:T(8,128)}), (f32[256,1024]{1,0:T(8,128)}, f32[1024,256]{1,0:T(8,128)})) %all-reduce.4.cloned.1.call-update) | async-done | bytes 2097168 | tf_op jit(solution)/shard_map/psum | solution.py:144
  339.4 2.4 broadcast_multiply_fusion.1
  341.8 1.0 broadcast_multiply_fusion
  (53 shorter events, 5.6 us)
Async XLA Ops:
  7.2 73.1 %copy-start = (bf16[256,1024]{1,0:T(8,128)(2,1)S(1)}, bf16[256,1024]{1,0:T(8,128)(2,1)}, u32[]{:S(2)}) copy-start(bf16[256,1024]{1,0:T(8,128)(2,1)} %param.18) | copy-start | bytes 1572868
  7.2 20.4 %copy-start.4 = (bf16[16,128,256]{2,1,0:T(8,128)(2,1)S(1)}, bf16[16,128,256]{2,1,0:T(8,128)(2,1)}, u32[]{:S(2)}) copy-start(bf16[16,128,256]{2,1,0:T(8,128)(2,1)} %param.11) | copy-start | bytes 3145732
  7.2 332.2 %all-reduce.4.cloned.1.call-start = ((), (), s32[]{:S(2)}) async-start(), calls=%async_computation | async-start | bytes 4194304 | tf_op jit(solution)/shard_map/psum | solution.py:144
  8.3 9.4 %collective-permute-start = (bf16[16,3,256]{2,1,0:T(4,128)(2,1)S(1)}, bf16[16,3,256]{2,1,0:T(4,128)(2,1)S(1)}, u32[]{:S(2)}, u32[]{:S(2)}) collective-permute-start(bf16[16,3,256]{2,1,0:T(4,128)(2,1)S(1)} %get-tuple-element.70), channel_id=1, source_target_pairs={{0,8},{8,16},{16,24},{24,32},{32,40},{40,48},{48,56},{56,64},{64,7... | collective-permute-start | bytes 73736 | tf_op jit(solution)/shard_map/ppermute | solution.py:23
  8.3 9.3 %collective-permute-start.1 = (bf16[16,3,256]{2,1,0:T(4,128)(2,1)S(1)}, bf16[16,3,256]{2,1,0:T(4,128)(2,1)S(1)}, u32[]{:S(2)}, u32[]{:S(2)}) collective-permute-start(bf16[16,3,256]{2,1,0:T(4,128)(2,1)S(1)} %get-tuple-element.71), channel_id=1, source_target_pairs={{8,0},{16,8},{24,16},{32,24},{40,32},{48,40},{56,48},{64,56},{72,6... | collective-permute-start | bytes 73736 | tf_op jit(solution)/shard_map/ppermute | solution.py:26
  18.8 8.9 %collective-permute-start.2 = (bf16[3,134,256]{2,1,0:T(8,128)(2,1)S(1)}, bf16[3,134,256]{2,1,0:T(8,128)(2,1)S(1)}, u32[]{:S(2)}, u32[]{:S(2)}) collective-permute-start(bf16[3,134,256]{2,1,0:T(8,128)(2,1)S(1)} %get-tuple-element.64), channel_id=1, source_target_pairs={{0,1},{1,2},{2,3},{3,4},{4,5},{5,6},{6,7},{7,0},{8,9},{9,10},{10,1... | collective-permute-start | bytes 617480 | tf_op jit(solution)/shard_map/ppermute | solution.py:23
  20.4 7.2 %collective-permute-start.3 = (bf16[3,134,256]{2,1,0:T(8,128)(2,1)S(1)}, bf16[3,134,256]{2,1,0:T(8,128)(2,1)S(1)}, u32[]{:S(2)}, u32[]{:S(2)}) collective-permute-start(bf16[3,134,256]{2,1,0:T(8,128)(2,1)S(1)} %get-tuple-element.65), channel_id=1, source_target_pairs={{1,0},{2,1},{3,2},{4,3},{5,4},{6,5},{7,6},{0,7},{9,8},{10,9},{11,1... | collective-permute-start | bytes 617480 | tf_op jit(solution)/shard_map/ppermute | solution.py:26
  78.8 0.7 copy-start.9
  78.9 0.7 copy-start.10
  79.5 0.8 copy-start.13
  80.3 3.7 %copy-start.12 = (bf16[1024,256]{1,0:T(8,128)(2,1)S(1)}, bf16[1024,256]{1,0:T(8,128)(2,1)}, u32[]{:S(2)}) copy-start(bf16[1024,256]{1,0:T(8,128)(2,1)} %param.20) | copy-start | bytes 1572868
  84.1 1.3 copy-start.5
  84.1 1.5 copy-start.6
  84.1 1.5 copy-start.11
  104.9 1.9 copy-start.1
  112.3 8.3 %copy-start.2 = (bf16[16,128,256]{2,1,0:T(8,128)(2,1)}, bf16[16,128,256]{2,1,0:T(8,128)(2,1)S(1)}, u32[]{:S(2)}) copy-start(bf16[16,128,256]{2,1,0:T(8,128)(2,1)S(1)} %get-tuple-element.59) | copy-start | bytes 3145732
  120.6 70.6 %copy-start.3 = (bf16[16,128,256]{2,1,0:T(8,128)(2,1)S(1)}, bf16[16,128,256]{2,1,0:T(8,128)(2,1)}, u32[]{:S(2)}) copy-start(bf16[16,128,256]{2,1,0:T(8,128)(2,1)} %copy-done.2) | copy-start | bytes 3145732
  120.8 70.4 %collective-permute-start.4 = (bf16[16,3,256]{2,1,0:T(4,128)(2,1)S(1)}, bf16[16,3,256]{2,1,0:T(4,128)(2,1)S(1)}, u32[]{:S(2)}, u32[]{:S(2)}) collective-permute-start(bf16[16,3,256]{2,1,0:T(4,128)(2,1)S(1)} %get-tuple-element.68), channel_id=1, source_target_pairs={{0,8},{8,16},{16,24},{24,32},{32,40},{40,48},{48,56},{56,64},{64,7... | collective-permute-start | bytes 73736 | tf_op jit(solution)/shard_map/ppermute | solution.py:23
  120.9 70.3 %collective-permute-start.5 = (bf16[16,3,256]{2,1,0:T(4,128)(2,1)S(1)}, bf16[16,3,256]{2,1,0:T(4,128)(2,1)S(1)}, u32[]{:S(2)}, u32[]{:S(2)}) collective-permute-start(bf16[16,3,256]{2,1,0:T(4,128)(2,1)S(1)} %get-tuple-element.69), channel_id=1, source_target_pairs={{8,0},{16,8},{24,16},{32,24},{40,32},{48,40},{56,48},{64,56},{72,6... | collective-permute-start | bytes 73736 | tf_op jit(solution)/shard_map/ppermute | solution.py:26
  191.3 9.2 %collective-permute-start.6 = (bf16[3,134,256]{2,1,0:T(8,128)(2,1)S(1)}, bf16[3,134,256]{2,1,0:T(8,128)(2,1)S(1)}, u32[]{:S(2)}, u32[]{:S(2)}) collective-permute-start(bf16[3,134,256]{2,1,0:T(8,128)(2,1)S(1)} %get-tuple-element.62), channel_id=1, source_target_pairs={{0,1},{1,2},{2,3},{3,4},{4,5},{5,6},{6,7},{7,0},{8,9},{9,10},{10,1... | collective-permute-start | bytes 617480 | tf_op jit(solution)/shard_map/ppermute | solution.py:23
  192.8 7.8 %collective-permute-start.7 = (bf16[3,134,256]{2,1,0:T(8,128)(2,1)S(1)}, bf16[3,134,256]{2,1,0:T(8,128)(2,1)S(1)}, u32[]{:S(2)}, u32[]{:S(2)}) collective-permute-start(bf16[3,134,256]{2,1,0:T(8,128)(2,1)S(1)} %get-tuple-element.63), channel_id=1, source_target_pairs={{1,0},{2,1},{3,2},{4,3},{5,4},{6,5},{7,6},{0,7},{9,8},{10,9},{11,1... | collective-permute-start | bytes 617480 | tf_op jit(solution)/shard_map/ppermute | solution.py:26
  196.1 6.6 %copy-start.7 = (bf16[16,128,256]{2,1,0:T(8,128)(2,1)S(1)}, bf16[16,128,256]{2,1,0:T(8,128)(2,1)}, u32[]{:S(2)}) copy-start(bf16[16,128,256]{2,1,0:T(8,128)(2,1)} %param.12) | copy-start | bytes 3145732
  339.4 2.4 copy-start.8
Sparse Core Ops, SparseCore 0:
  191.3 148.0 all-reduce.3
where the time goes:
time: 351 us; the launch traced here: 350 us
  other arithmetic  129 us (37%)
  waiting for transfers between devices  95 us (27%)
  blocking collectives  64.3 us (18%)
  matrix products  22.4 us (6%)
  starting transfers between devices  19.7 us (6%)
  between operations  14.4 us (4%)
  local copies, waits for them, and re-layouts  5.25 us (1%)
    psum x1, waiting for transfers between devices, on_device(): lax.psum((grad_wi, grad_wo, kernel_sum, scale_sum), ('lon', 'lat'))  86.8 us
    psum x1, blocking collectives, on_device(): lax.psum((grad_wi, grad_wo, kernel_sum, scale_sum), ('lon', 'lat'))  64.3 us
    convert_element_type x1, other arithmetic, on_device(): grad_features.astype(jnp.bfloat16)  49.9 us
    reduce_sum x1, other arithmetic, on_device(): row_mean = jnp.mean(mixed, axis=-1, keepdims=True)  49 us
    ppermute x4, starting transfers between devices, padded_2(): lax.ppermute(lax.slice_in_dim(block, 0, width, axis=dim), axis, backward)  16.4 us
    reduce_sum x3, other arithmetic, on_device(): jnp.sum(grad_wide * padded[row_off:row_off + rows, col_off:col_off + tile...  13.8 us
    ppermute x4, waiting for transfers between devices, padded_2(): lax.ppermute(lax.slice_in_dim(block, block.shape[dim] - width, None, axis...  8.24 us
    dot_general x1, matrix products, pointwise(): grad_act = jnp.dot(grad_rows, w_out.T, preferred_element_type=jnp.float32)  7.17 us
  transfers between devices with their start and end apart: 9, of which 3 were waited for; matrix products, arithmetic and copies ran while one was open for 17% of the time, Pallas kernels for 0%

commit v1 on v0

v1 whole, which is shorter than its diff:
```python
import math

import jax
import jax.numpy as jnp
from jax import lax
from jax.experimental import pallas as pl
from jax.experimental.pallas import tpu as pltpu
from jax.sharding import Mesh
from jax.sharding import PartitionSpec as P

KS = 7
MARGIN = KS // 2
HALF = 128
STEP = 8
SPAN = 16
EDGE = 8
TAPS = (KS + 1) // 2 * KS
GELU_SCALE = math.sqrt(2.0 / math.pi)
GELU_CUBE = 0.044715
EPSILON = 1e-06
LON = ("x", "zh", "core")
LAT = ("zl", "y")
CHIPS = ("x", "zh", "zl", "y")
ALL = ("x", "zh", "core", "zl", "y")
F32 = jnp.float32
BF16 = jnp.bfloat16


def dot(a, b):
    return jnp.dot(a, b, preferred_element_type=F32)


def dot_cells(a, b):
    return lax.dot_general(a, b, (((0,), (0,)), ((), ())), preferred_element_type=F32)


def build_weights(taps_ref, w_ref, flip):
    rows = lax.broadcasted_iota(jnp.int32, (HALF, HALF), 0)
    cols = lax.broadcasted_iota(jnp.int32, (HALF, HALF), 1)
    eye = rows == cols
    zero = jnp.zeros((HALF, HALF), F32)
    for h in range(2):
        for i2 in range((KS + 1) // 2):
            for j in range(KS):
                tile = i2 * KS + j
                for a in range(2):
                    for b in range(2):
                        i = 2 * i2 + a - b
                        if 0 <= i < KS:
                            tap = (KS - 1 - i) * KS + (KS - 1 - j) if flip else i * KS + j
                            row = taps_ref[tap : tap + 1, h * HALF : (h + 1) * HALF]
                            block = jnp.where(eye, row, zero)
                        else:
                            block = zero
                        w_ref[
                            h,
                            tile * 256 + a * HALF : tile * 256 + (a + 1) * HALF,
                            b * HALF : (b + 1) * HALF,
                        ] = block.astype(BF16)


def assemble(flag_ref, main_ref, west_ref, east_ref, south_ref, north_ref, wide, xs, xs_wide):
    rows, tile, _ = main_ref.shape
    for h in range(2):
        lanes = slice(h * HALF, (h + 1) * HALF)
        wide[h, 0:MARGIN] = south_ref[:, :, lanes].astype(F32) * flag_ref[0, 0]
        wide[h, rows + MARGIN : rows + 2 * MARGIN] = (
            north_ref[:, :, lanes].astype(F32) * flag_ref[0, 1]
        )

        def place(r, _):
            wide[h, r + MARGIN, EDGE : EDGE + tile, :] = main_ref[r, :, lanes].astype(F32)
            wide[h, r + MARGIN, 0:EDGE, :] = west_ref[r, :, lanes].astype(F32)
            wide[h, r + MARGIN, EDGE + tile : 2 * EDGE + tile, :] = east_ref[r, :, lanes].astype(
                F32
            )
            return 0

        lax.fori_loop(0, rows, place, 0)

        def spread(r, _):
            for t in range(STEP + 2 * MARGIN):
                piece = wide[h, r, pl.ds(EDGE - MARGIN + t, SPAN, stride=STEP), :]
                if xs_wide is not None:
                    xs_wide[h, r, t] = piece
                xs[h, r, t] = piece.astype(BF16)
            return 0

        lax.fori_loop(0, rows + 2 * MARGIN, spread, 0)


def conv_pair(xs, w_ref, h, pair):
    pieces = []
    for i2 in range((KS + 1) // 2):
        for j in range(KS):
            for a in range(2):
                pieces.append(
                    xs[h, 2 * pair + 2 * i2 + a, j : j + STEP].reshape(STEP * SPAN, HALF)
                )
    return dot(jnp.concatenate(pieces, axis=1), w_ref[h])


def forward_kernel(
    flag_ref,
    main_ref,
    west_ref,
    east_ref,
    south_ref,
    north_ref,
    cot_ref,
    mask_ref,
    taps_ref,
    gain_ref,
    bias_ref,
    w_in_ref,
    w_in_t_ref,
    b_in_ref,
    w_out_ref,
    w_out_t_ref,
    scale_ref,
    out_ref,
    gm_ref,
    sums_ref,
    wide,
    xs,
    xs_wide,
    w_ref,
    out_wide,
    gm_wide,
    gm_xs,
    acc_in,
    acc_out,
    acc_scale,
):
    rows = main_ref.shape[0]
    ff = w_in_ref.shape[1]
    width = 2 * HALF
    cells = 2 * STEP * SPAN
    build_weights(taps_ref, w_ref, False)
    assemble(flag_ref, main_ref, west_ref, east_ref, south_ref, north_ref, wide, xs, xs_wide)
    acc_in[...] = jnp.zeros_like(acc_in)
    acc_out[...] = jnp.zeros_like(acc_out)
    acc_scale[...] = jnp.zeros_like(acc_scale)
    gain, bias, scale = gain_ref[...], bias_ref[...], scale_ref[...]

    def pair_step(pair, _):
        low = conv_pair(xs, w_ref, 0, pair)
        high = conv_pair(xs, w_ref, 1, pair)
        mixed = jnp.concatenate(
            [
                jnp.concatenate([low[:, :HALF], high[:, :HALF]], axis=1),
                jnp.concatenate([low[:, HALF:], high[:, HALF:]], axis=1),
            ],
            axis=0,
        )
        mean = jnp.mean(mixed, axis=1, keepdims=True)
        centered = mixed - mean
        var = jnp.mean(centered * centered, axis=1, keepdims=True)
        inverse = lax.rsqrt(var + EPSILON)
        normed = centered * inverse
        normalized = (normed * gain + bias).astype(BF16)
        cot = cot_ref[pl.ds(2 * pair, 2)].reshape(cells, width).astype(F32)
        grad_out = (cot * scale).astype(BF16)
        branch = jnp.zeros((cells, width), F32)
        grad_norm = jnp.zeros((cells, width), F32)
        for f in range(ff // 256):
            part = slice(f * 256, (f + 1) * 256)
            hidden = dot(normalized, w_in_ref[:, part]) + b_in_ref[:, part]
            square = hidden * hidden
            hyper = jnp.tanh(hidden * (GELU_SCALE + GELU_SCALE * GELU_CUBE * square))
            gate = 0.5 + 0.5 * hyper
            act = hidden * gate
            slope = gate + act * (1.0 - gate) * (
                2.0 * GELU_SCALE + 6.0 * GELU_SCALE * GELU_CUBE * square
            )
            act_low = act.astype(BF16)
            grad_hidden = (dot(grad_out, w_out_t_ref[:, part]) * slope).astype(BF16)
            branch = branch + dot(act_low, w_out_ref[part, :])
            grad_norm = grad_norm + dot(grad_hidden, w_in_t_ref[part, :])
            acc_in[:, part] += dot_cells(normalized, grad_hidden)
            acc_out[:, part] += dot_cells(grad_out, act_low)
        branch = branch.astype(BF16).astype(F32)
        acc_scale[...] += jnp.sum((cot * branch).reshape(cells // 8, 8, width), axis=0)
        g = grad_norm.astype(BF16).astype(F32) * gain
        grad_mixed = inverse * (
            g
            - jnp.mean(g, axis=1, keepdims=True)
            - normed * jnp.mean(g * normed, axis=1, keepdims=True)
        )
        grad_mixed = grad_mixed.astype(BF16).astype(F32)
        mask = mask_ref[pl.ds(2 * pair, 2)].reshape(cells, HALF).astype(F32)
        for h in range(2):
            lanes = slice(h * HALF, (h + 1) * HALF)
            added = mask * scale[:, lanes] * branch[:, lanes]
            for b in range(2):
                row = 2 * pair + b
                for t in range(STEP):
                    start = b * STEP * SPAN + t * SPAN
                    feature = xs_wide[h, row + MARGIN, t + MARGIN]
                    out_wide[h, row, pl.ds(t, SPAN, stride=STEP), :] = (
                        feature + added[start : start + SPAN]
                    )
                    piece = grad_mixed[start : start + SPAN, lanes]
                    gm_wide[h, row, pl.ds(t, SPAN, stride=STEP), :] = piece
                    gm_xs[h, row, t] = piece
        return 0

    lax.fori_loop(0, rows // 2, pair_step, 0)

    def finish(r, _):
        for h in range(2):
            lanes = slice(h * HALF, (h + 1) * HALF)
            out_ref[r, :, lanes] = out_wide[h, r].astype(BF16)
            gm_ref[r, :, lanes] = gm_wide[h, r].astype(BF16)
        return 0

    lax.fori_loop(0, rows, finish, 0)
    half_ff = ff // 2
    groups = width // 8

    def pack(group, _):
        for which, acc in enumerate((acc_in, acc_out)):
            for side in range(2):
                sums_ref[which * 2 * groups + group * 2 + side, :, 0:half_ff] = acc[
                    pl.ds(pl.multiple_of(group * 8, 8), 8), side * half_ff : (side + 1) * half_ff
                ].astype(BF16)
        return 0

    lax.fori_loop(0, groups, pack, 0)
    for spot in range(2 * (KS * KS + 1), sums_ref.shape[0]):
        sums_ref[spot, :, half_ff:] = jnp.zeros((8, HALF), BF16)
    for h in range(2):
        lanes = slice(h * HALF, (h + 1) * HALF)
        sums_ref[2 * KS * KS + h, :, half_ff:] = acc_scale[:, lanes].astype(BF16)

        def tap_step(r, sums):
            sums = list(sums)
            for t in range(STEP):
                for side in range(2):
                    part = slice(side * 8, side * 8 + 8)
                    g = gm_xs[h, r, t, part]
                    for i in range(KS):
                        for j in range(KS):
                            sums[i * KS + j] = sums[i * KS + j] + g * xs_wide[h, r + i, t + j, part]
            return tuple(sums)

        sums = lax.fori_loop(
            0, rows, tap_step, tuple(jnp.zeros((8, HALF), F32) for _ in range(KS * KS))
        )
        for tap in range(KS * KS):
            sums_ref[2 * tap + h, :, half_ff:] = sums[tap].astype(BF16)


def backward_kernel(
    flag_ref,
    main_ref,
    west_ref,
    east_ref,
    south_ref,
    north_ref,
    cot_ref,
    taps_ref,
    out_ref,
    wide,
    xs,
    w_ref,
    out_wide,
):
    rows = main_ref.shape[0]
    build_weights(taps_ref, w_ref, True)
    assemble(flag_ref, main_ref, west_ref, east_ref, south_ref, north_ref, wide, xs, None)

    def pair_step(pair, _):
        for h in range(2):
            lanes = slice(h * HALF, (h + 1) * HALF)
            both = conv_pair(xs, w_ref, h, pair)
            for b in range(2):
                for t in range(STEP):
                    out_wide[h, 2 * pair + b, pl.ds(t, SPAN, stride=STEP), :] = both[
                        t * SPAN : (t + 1) * SPAN, b * HALF : (b + 1) * HALF
                    ]
                row = 2 * pair + b
                out_ref[row, :, lanes] = (
                    cot_ref[row, :, lanes].astype(F32) + out_wide[h, row]
                ).astype(BF16)
        return 0

    lax.fori_loop(0, rows // 2, pair_step, 0)


def rim(field):
    rows, tile, width = field.shape
    gap = jnp.zeros((rows, EDGE - MARGIN, width), BF16)
    count = lax.axis_size(LON)
    forward = [(i, (i + 1) % count) for i in range(count)]
    backward = [(i, (i - 1) % count) for i in range(count)]
    west = lax.ppermute(field[:, tile - MARGIN :], LON, forward)
    east = lax.ppermute(field[:, :MARGIN], LON, backward)
    west = jnp.concatenate([gap, west], axis=1)
    east = jnp.concatenate([east, gap], axis=1)
    full = jnp.concatenate([west, field, east], axis=1)
    count = lax.axis_size(LAT)
    forward = [(i, (i + 1) % count) for i in range(count)]
    backward = [(i, (i - 1) % count) for i in range(count)]
    south = lax.ppermute(full[rows - MARGIN :], LAT, forward)
    north = lax.ppermute(full[:MARGIN], LAT, backward)
    return west, east, south, north


def on_device(
    features, cotangent, land_sea, tile_slot, kernel, ln_gain, ln_bias, w_in, b_in, w_out, layer_scale
):
    rows, tile, width = features.shape
    ff = w_in.shape[1]
    devices = lax.axis_size(ALL)
    slot_total = 64
    band = lax.axis_index(LAT)
    flags = jnp.stack([band > 0, band < lax.axis_size(LAT) - 1]).astype(F32).reshape(1, 2)
    taps = kernel.reshape(KS * KS, width)
    mask = (tile_slot < slot_total) & (land_sea > 0)
    cot_masked = jnp.where(mask[:, :, None], cotangent, jnp.zeros_like(cotangent))
    cot_masked = cot_masked.reshape(rows, SPAN, STEP, width).transpose(0, 2, 1, 3)
    mask_wide = jnp.broadcast_to(
        mask.reshape(rows, SPAN, STEP).transpose(0, 2, 1)[..., None].astype(BF16),
        (rows, STEP, SPAN, HALF),
    )
    padded = rows + 2 * MARGIN
    ext = STEP + 2 * MARGIN
    vmem = pl.BlockSpec(memory_space=pltpu.VMEM)
    smem = pl.BlockSpec(memory_space=pltpu.SMEM)
    params = pltpu.CompilerParams(vmem_limit_bytes=56 * 1024 * 1024)
    wide = pltpu.VMEM((2, padded, tile + 2 * EDGE, HALF), F32)
    xs = pltpu.VMEM((2, padded, ext, SPAN, HALF), BF16)
    weights = pltpu.VMEM((2, TAPS * 256, 256), BF16)
    flat = pltpu.VMEM((2, rows, tile, HALF), F32)
    west, east, south, north = rim(features)
    chunk = ff // 2 + HALF
    output, grad_mixed, sums = pl.pallas_call(
        forward_kernel,
        out_shape=(
            jax.ShapeDtypeStruct(features.shape, BF16),
            jax.ShapeDtypeStruct(features.shape, BF16),
            jax.ShapeDtypeStruct((devices, 8, chunk), BF16),
        ),
        in_specs=[smem] + [vmem] * 16,
        out_specs=(vmem, vmem, vmem),
        scratch_shapes=[
            wide,
            xs,
            pltpu.VMEM((2, padded, ext, SPAN, HALF), F32),
            weights,
            flat,
            flat,
            pltpu.VMEM((2, rows, STEP, SPAN, HALF), F32),
            pltpu.VMEM((width, ff), F32),
            pltpu.VMEM((width, ff), F32),
            pltpu.VMEM((8, width), F32),
        ],
        compiler_params=params,
        cost_estimate=pl.CostEstimate(
            flops=14_000_000_000, bytes_accessed=8_000_000, transcendentals=2_000_000
        ),
        name="forward",
    )(
        flags,
        features,
        west,
        east,
        south,
        north,
        cot_masked,
        mask_wide,
        taps,
        ln_gain.reshape(1, width),
        ln_bias.reshape(1, width),
        w_in,
        w_in.T,
        b_in.reshape(1, ff),
        w_out,
        w_out.T,
        layer_scale.reshape(1, width),
    )
    west, east, south, north = rim(grad_mixed)
    arrived = lax.all_to_all(sums, ALL, split_axis=0, concat_axis=0, tiled=True)
    grad_features = pl.pallas_call(
        backward_kernel,
        out_shape=jax.ShapeDtypeStruct(features.shape, BF16),
        in_specs=[smem] + [vmem] * 7,
        out_specs=vmem,
        scratch_shapes=[wide, xs, weights, flat],
        compiler_params=params,
        cost_estimate=pl.CostEstimate(
            flops=7_000_000_000, bytes_accessed=4_000_000, transcendentals=0
        ),
        name="backward",
    )(flags, grad_mixed, west, east, south, north, cotangent, taps)
    own = jnp.sum(arrived.astype(F32), axis=0).astype(BF16)
    chips = lax.axis_size(CHIPS)
    mine = lax.all_to_all(
        jnp.broadcast_to(own[None], (chips,) + own.shape), CHIPS, split_axis=0, concat_axis=0, tiled=True
    )
    other = lax.ppermute(mine, "core", [(0, 1), (1, 0)])
    first = lax.axis_index("core") == 0
    pair = jnp.stack([jnp.where(first, mine, other), jnp.where(first, other, mine)])
    outer = lax.axis_size(("x", "zh"))
    whole = pair.reshape(2, outer, chips // outer, 8, chunk).transpose(1, 0, 2, 3, 4)
    whole = whole.reshape(devices, 8, chunk)
    factor = 1.0 / math.sqrt(rows * lax.axis_size(LAT) * tile * lax.axis_size(LON))
    main = whole[:, :, : ff // 2].reshape(2, width // 8, 2, 8, ff // 2)
    main = main.transpose(0, 1, 3, 2, 4).reshape(2, width, ff).astype(F32) * factor
    small = jnp.sum(whole[: 2 * (KS * KS + 1), :, ff // 2 :].astype(F32), axis=1) * factor
    small = small.reshape(KS * KS + 1, width)
    return (
        output,
        grad_features,
        main[0],
        main[1].T,
        small[: KS * KS].reshape(KS, KS, width),
        small[KS * KS],
    )


def solution(mesh):
    fine = Mesh(mesh.devices.reshape(4, 2, 2, 2, 4), ("x", "zh", "core", "zl", "y"))
    cells = P(LAT, LON, None)
    return jax.shard_map(
        on_device,
        mesh=fine,
        in_specs=(cells, cells, P(LAT, LON), P(LAT, LON)) + (P(),) * 7,
        out_specs=(cells, cells, P(), P(), P(), P()),
        check_vma=False,
    )
```

time: 351 us -> 147 us (0.42)
  other arithmetic: 129 us -> 4.73 us
  waiting for transfers between devices: 95 us -> 19.8 us
  Pallas kernels: 0 us -> 52.3 us
  blocking collectives: 64.3 us -> 28 us
  matrix products: 22.4 us -> 0 us
  local copies, waits for them, and re-layouts: 5.25 us -> 19.8 us
  between operations: 14.4 us -> 0.77 us
    psum x1 -> x0, waiting for transfers between devices: 86.8 us -> none  [on_device(): lax.psum((grad_wi, grad_wo, kernel_sum, scale_sum), ('lon', 'lat'))]
    reduce_sum x7 -> x2, other arithmetic: 66.3 us -> 0.37 us  [the longest x1 0.24 us: on_device(): own = jnp.sum(arrived.astype(F32), axis=0).astype(BF16)]
    psum x1 -> x0, blocking collectives: 64.3 us -> none  [on_device(): lax.psum((grad_wi, grad_wo, kernel_sum, scale_sum), ('lon', 'lat'))]
    convert_element_type x4 -> x2, other arithmetic: 55 us -> 1.98 us  [the longest x1 1.37 us: on_device(): mask.reshape(rows, SPAN, STEP).transpose(0, 2, 1)[..., None].astype(BF16)]
    pallas_call x0 -> x2, Pallas kernels: none -> 52.3 us  [the longest x1 37.9 us: on_device(): pl.pallas_call(forward_kernel, out_shape=(jax.ShapeDtypeStruct(features.s...]
    all_to_all x0 -> x1, blocking collectives: none -> 28 us  [on_device(): arrived = lax.all_to_all(sums, ALL, split_axis=0, concat_axis=0, tiled=True)]
    dot_general x6 -> x0, matrix products: 22.4 us -> none  [the longest x1 7.17 us: pointwise(): grad_act = jnp.dot(grad_rows, w_out.T, preferred_element_type=jnp.float32)]
    ppermute x8 -> x9, waiting for transfers between devices: 8.25 us -> 19.8 us  [the longest x2 11.1 us: rim(): west = lax.ppermute(field[:, tile - MARGIN:], LON, forward)]
  transfers between devices with their start and end apart: 9 -> 10, of which waited for: 3 -> 6; matrix products, arithmetic and copies ran while one was open for 17% -> 8% of each run, Pallas kernels for 0% -> 10%
where the time goes in v1:
time: 147 us
  Pallas kernels  52.3 us (36%)
  blocking collectives  28 us (19%)
  starting transfers between devices  21.1 us (14%)
  local copies, waits for them, and re-layouts  19.8 us (13%)
  waiting for transfers between devices  19.8 us (13%)
  other arithmetic  4.73 us (3%)
    pallas_call x1, Pallas kernels, on_device(): pl.pallas_call(forward_kernel, out_shape=(jax.ShapeDtypeStruct(features.s...  37.9 us
    all_to_all x1, blocking collectives, on_device(): arrived = lax.all_to_all(sums, ALL, split_axis=0, concat_axis=0, tiled=True)  28 us
    pallas_call x1, Pallas kernels, on_device(): pl.pallas_call(backward_kernel, out_shape=jax.ShapeDtypeStruct(features.s...  14.4 us
    ppermute x2, waiting for transfers between devices, rim(): west = lax.ppermute(field[:, tile - MARGIN:], LON, forward)  11.1 us
    ppermute x2, starting transfers between devices, rim(): east = lax.ppermute(field[:, :MARGIN], LON, backward)  10.2 us
    ppermute x2, starting transfers between devices, rim(): north = lax.ppermute(full[:MARGIN], LAT, backward)  6.22 us
    ppermute x2, waiting for transfers between devices, rim(): south = lax.ppermute(full[rows - MARGIN:], LAT, forward)  4.83 us
    all_to_all x1, starting transfers between devices, on_device(): lax.all_to_all(jnp.broadcast_to(own[None], (chips,) + own.shape), CHIPS,...  4.64 us
  transfers between devices with their start and end apart: 10, of which 6 were waited for; matrix products, arithmetic and copies ran while one was open for 8% of the time, Pallas kernels for 10%

profile of v1, /device:TPU:0, one launch (start us, length us, event | category | flops | bytes accessed | tf_op | source)
XLA Modules:
  0.0 146.5 jit_solution(14816531325464363280)
XLA Ops:
  0.6 0.9 fusion.5
  1.5 5.7 %collective-permute-start.1 = (bf16[16,3,256]{2,1,0:T(4,128)(2,1)S(1)}, bf16[16,3,256]{2,1,0:T(4,128)(2,1)S(1)}, u32[]{:S(2)}, u32[]{:S(2)}) collective-permute-start(bf16[16,3,256]{2,1,0:T(4,128)(2,1)S(1)} %get-tuple-element.36), channel_id=1, source_target_pairs={{0,120},{8,0},{16,8},{24,16},{32,24},{40,32},{48,40},{56,48},{64,5... | collective-permute-start | bytes 73736 | tf_op jit(solution)/shard_map/ppermute | solution.py:298
  7.2 0.7 compare_bitcast_fusion
  7.9 1.4 fusion
  9.2 4.9 %collective-permute-done = bf16[16,3,256]{2,1,0:T(4,128)(2,1)S(1)} collective-permute-done((bf16[16,3,256]{2,1,0:T(4,128)(2,1)S(1)}, bf16[16,3,256]{2,1,0:T(4,128)(2,1)S(1)}, u32[]{:S(2)}, u32[]{:S(2)}) %collective-permute-start) | collective-permute-done | bytes 24608 | tf_op jit(solution)/shard_map/ppermute | solution.py:297
  14.2 3.9 %concatenate.30 = bf16[16,144,256]{2,1,0:T(8,128)(2,1)S(1)} concatenate(bf16[16,5,256]{2,1,0:T(8,128)(2,1)S(1)} %broadcast.23, bf16[16,3,256]{2,1,0:T(4,128)(2,1)S(1)} %collective-permute-done, bf16[16,128,256]{2,1,0:T(8,128)(2,1)} %main_ref.1, bf16[16,3,256]{2,1,0:T(4,128)(2,1)S(1)} %collective-permute-done.1, bf16[16,5,256]{2,1,0:T(8,128)(2,1)S(1)} %broadcast.23), dimensions={1} | concatenate | bytes 2359296 | tf_op jit(solution)/shard_map/concatenate | solution.py:301
  18.1 0.7 fusion.3
  18.8 3.5 %collective-permute-start.3 = (bf16[3,144,256]{2,1,0:T(8,128)(2,1)}, bf16[3,144,256]{2,1,0:T(8,128)(2,1)}, u32[]{:S(2)}, u32[]{:S(2)}) collective-permute-start(bf16[3,144,256]{2,1,0:T(8,128)(2,1)} %get-tuple-element.32), channel_id=1, source_target_pairs={{0,7},{1,0},{2,1},{3,2},{4,3},{5,4},{6,5},{7,6},{8,15},{9,8},{10,9... | collective-permute-start | bytes 663560 | tf_op jit(solution)/shard_map/ppermute | solution.py:306
  22.3 1.2 select_bitcast_fusion
  23.5 0.8 copy.30
  25.1 1.0 copy.32
  26.1 1.0 copy.33
  27.1 1.2 copy.36
  28.9 0.6 concatenate.28.west_ref
  29.6 0.6 concatenate.29.east_ref
  30.5 1.1 broadcast_in_dim.26.mask_ref
  31.6 37.9 %forward.1 = (bf16[16,128,256]{2,1,0:T(8,128)(2,1)}, bf16[16,128,256]{2,1,0:T(8,128)(2,1)}, bf16[128,8,640]{2,1,0:T(8,128)(2,1)}) custom-call(f32[1,2]{1,0:T(1,128)} %add_convert_fusion.flag_ref, bf16[16,128,256]{2,1,0:T(8,128)(2,1)} %main_ref.1, bf16[16,8,256]{2,1,0:T(8,128)(2,1)} %concatenate.28.west_ref, bf16[16,8,256]{2,1,0:T(8,128)(2,1)} %concatenate.29.east_ref, ...), custom_call_target="tpu_custom_call" | custom-call | flops 14000000000 | bytes 8000000 | tf_op jit(solution)/shard_map/forward/pallas_call | solution.py:338
  69.5 28.0 %all_to_all.10 = bf16[128,8,640]{2,1,0:T(8,128)(2,1)S(1)} all-to-all(bf16[128,8,640]{2,1,0:T(8,128)(2,1)} %get-tuple-element.11), channel_id=1, replica_groups=mesh['x'=4,'zh'=2,'core'=2,'zl'=2,'y'=4] {'x','zh','core','zl','y'}, dimensions={0} | all-to-all | bytes 2621440 | tf_op jit(solution)/shard_map/all_to_all | solution.py:384
  97.7 0.9 broadcast_in_dim.27
  98.6 4.6 %all-to-all-start.1 = ((bf16[64,8,640]{2,1,0:T(8,128)(2,1)}), bf16[64,8,640]{2,1,0:T(8,128)(2,1)S(1)}, u32[]{:S(2)}, u32[]{:S(2)}) async-start(bf16[64,8,640]{2,1,0:T(8,128)(2,1)} %broadcast_in_dim.27), calls=%async_computation.1 | async-start | bytes 1310720 | tf_op jit(solution)/shard_map/all_to_all | solution.py:399
  103.3 4.5 %collective-permute-start.5 = (bf16[16,3,256]{2,1,0:T(4,128)(2,1)S(1)}, bf16[16,3,256]{2,1,0:T(4,128)(2,1)S(1)}, u32[]{:S(2)}, u32[]{:S(2)}) collective-permute-start(bf16[16,3,256]{2,1,0:T(4,128)(2,1)S(1)} %get-tuple-element.34), channel_id=1, source_target_pairs={{0,120},{8,0},{16,8},{24,16},{32,24},{40,32},{48,40},{56,48},{64,5... | collective-permute-start | bytes 73736 | tf_op jit(solution)/shard_map/ppermute | solution.py:298
  107.9 1.8 %collective-permute-done.5 = bf16[16,3,256]{2,1,0:T(4,128)(2,1)S(1)} collective-permute-done((bf16[16,3,256]{2,1,0:T(4,128)(2,1)S(1)}, bf16[16,3,256]{2,1,0:T(4,128)(2,1)S(1)}, u32[]{:S(2)}, u32[]{:S(2)}) %collective-permute-start.5) | collective-permute-done | bytes 24608 | tf_op jit(solution)/shard_map/ppermute | solution.py:298
  109.6 6.2 %collective-permute-done.4 = bf16[16,3,256]{2,1,0:T(4,128)(2,1)S(1)} collective-permute-done((bf16[16,3,256]{2,1,0:T(4,128)(2,1)S(1)}, bf16[16,3,256]{2,1,0:T(4,128)(2,1)S(1)}, u32[]{:S(2)}, u32[]{:S(2)}) %collective-permute-start.4) | collective-permute-done | bytes 24608 | tf_op jit(solution)/shard_map/ppermute | solution.py:297
  116.2 2.8 %collective-permute-start.7 = (bf16[3,144,256]{2,1,0:T(8,128)(2,1)S(1)}, bf16[3,144,256]{2,1,0:T(8,128)(2,1)S(1)}, u32[]{:S(2)}, u32[]{:S(2)}) collective-permute-start(bf16[3,144,256]{2,1,0:T(8,128)(2,1)S(1)} %get-tuple-element.30), channel_id=1, source_target_pairs={{0,7},{1,0},{2,1},{3,2},{4,3},{5,4},{6,5},{7,6},{8,15},{9,8},{10,9... | collective-permute-start | bytes 663560 | tf_op jit(solution)/shard_map/ppermute | solution.py:306
  118.9 0.6 concatenate.31.west_ref
  119.6 0.6 concatenate.32.east_ref
  120.2 2.2 %collective-permute-done.7.north_ref = bf16[3,144,256]{2,1,0:T(8,128)(2,1)S(1)} collective-permute-done((bf16[3,144,256]{2,1,0:T(8,128)(2,1)S(1)}, bf16[3,144,256]{2,1,0:T(8,128)(2,1)S(1)}, u32[]{:S(2)}, u32[]{:S(2)}) %collective-permute-start.7) | collective-permute-done | bytes 221216 | tf_op jit(solution)/shard_map/ppermute | solution.py:306
  122.4 4.6 %collective-permute-done.6.south_ref = bf16[3,144,256]{2,1,0:T(8,128)(2,1)S(1)} collective-permute-done((bf16[3,144,256]{2,1,0:T(8,128)(2,1)S(1)}, bf16[3,144,256]{2,1,0:T(8,128)(2,1)S(1)}, u32[]{:S(2)}, u32[]{:S(2)}) %collective-permute-start.6) | collective-permute-done | bytes 221216 | tf_op jit(solution)/shard_map/ppermute | solution.py:305
  127.0 0.7 copy-done.6
  127.7 14.4 %backward.1 = bf16[16,128,256]{2,1,0:T(8,128)(2,1)} custom-call(f32[1,2]{1,0:T(1,128)} %add_convert_fusion.flag_ref, bf16[16,128,256]{2,1,0:T(8,128)(2,1)} %get-tuple-element.10.main_ref, bf16[16,8,256]{2,1,0:T(8,128)(2,1)} %concatenate.31.west_ref, bf16[16,8,256]{2,1,0:T(8,128)(2,1)} %concatenate.32.east_ref, bf16[3,144,256]{2,1,0:T(8,128)(2,1)} %copy-done.6, ...), custom_call_target="tpu_custom_call" | custom-call | flops 7000000000 | bytes 4000000 | tf_op jit(solution)/shard_map/backward/pallas_call | solution.py:385
  144.0 1.2 fusion.1
  145.2 1.3 copy.34
  (38 shorter events, 4.2 us)
Async XLA Ops:
  1.5 7.7 %collective-permute-start.1 = (bf16[16,3,256]{2,1,0:T(4,128)(2,1)S(1)}, bf16[16,3,256]{2,1,0:T(4,128)(2,1)S(1)}, u32[]{:S(2)}, u32[]{:S(2)}) collective-permute-start(bf16[16,3,256]{2,1,0:T(4,128)(2,1)S(1)} %get-tuple-element.36), channel_id=1, source_target_pairs={{0,120},{8,0},{16,8},{24,16},{32,24},{40,32},{48,40},{56,48},{64,5... | collective-permute-start | bytes 73736 | tf_op jit(solution)/shard_map/ppermute | solution.py:298
  7.2 7.0 %collective-permute-start = (bf16[16,3,256]{2,1,0:T(4,128)(2,1)S(1)}, bf16[16,3,256]{2,1,0:T(4,128)(2,1)S(1)}, u32[]{:S(2)}, u32[]{:S(2)}) collective-permute-start(bf16[16,3,256]{2,1,0:T(4,128)(2,1)S(1)} %get-tuple-element.37), channel_id=1, source_target_pairs={{0,8},{8,16},{16,24},{24,32},{32,40},{40,48},{48,56},{56,64},{64,7... | collective-permute-start | bytes 73736 | tf_op jit(solution)/shard_map/ppermute | solution.py:297
  14.2 8.1 %copy-start.1 = (bf16[16,128,256]{2,1,0:T(8,128)(2,1)S(1)}, bf16[16,128,256]{2,1,0:T(8,128)(2,1)}, u32[]{:S(2)}) copy-start(bf16[16,128,256]{2,1,0:T(8,128)(2,1)} %cot_ref.1) | copy-start | bytes 3145732
  18.8 5.6 %copy-start.4 = (f32[7,7,256]{2,1,0:T(8,128)S(1)}, f32[7,7,256]{2,1,0:T(8,128)}, u32[]{:S(2)}) copy-start(f32[7,7,256]{2,1,0:T(8,128)} %param.15) | copy-start | bytes 150532
  18.8 6.2 %copy-start.2 = (bf16[256,1024]{1,0:T(8,128)(2,1)S(1)}, bf16[256,1024]{1,0:T(8,128)(2,1)}, u32[]{:S(2)}) copy-start(bf16[256,1024]{1,0:T(8,128)(2,1)} %w_in_ref.1) | copy-start | bytes 1572868
  18.8 11.4 %collective-permute-start.3 = (bf16[3,144,256]{2,1,0:T(8,128)(2,1)}, bf16[3,144,256]{2,1,0:T(8,128)(2,1)}, u32[]{:S(2)}, u32[]{:S(2)}) collective-permute-start(bf16[3,144,256]{2,1,0:T(8,128)(2,1)} %get-tuple-element.32), channel_id=1, source_target_pairs={{0,7},{1,0},{2,1},{3,2},{4,3},{5,4},{6,5},{7,6},{8,15},{9,8},{10,9... | collective-permute-start | bytes 663560 | tf_op jit(solution)/shard_map/ppermute | solution.py:306
  22.3 8.1 %collective-permute-start.2 = (bf16[3,144,256]{2,1,0:T(8,128)(2,1)S(1)}, bf16[3,144,256]{2,1,0:T(8,128)(2,1)}, u32[]{:S(2)}, u32[]{:S(2)}) collective-permute-start(bf16[3,144,256]{2,1,0:T(8,128)(2,1)S(1)} %get-tuple-element.33), channel_id=1, source_target_pairs={{0,1},{1,2},{2,3},{3,4},{4,5},{5,6},{6,7},{7,0},{8,9},{9,10},{10,1... | collective-permute-start | bytes 663560 | tf_op jit(solution)/shard_map/ppermute | solution.py:305
  22.3 3.8 %copy-start.3 = (bf16[1024,256]{1,0:T(8,128)(2,1)S(1)}, bf16[1024,256]{1,0:T(8,128)(2,1)}, u32[]{:S(2)}) copy-start(bf16[1024,256]{1,0:T(8,128)(2,1)} %w_out_ref.1) | copy-start | bytes 1572868
  97.7 5.5 %copy-start = (bf16[16,128,256]{2,1,0:T(8,128)(2,1)S(1)}, bf16[16,128,256]{2,1,0:T(8,128)(2,1)}, u32[]{:S(2)}) copy-start(bf16[16,128,256]{2,1,0:T(8,128)(2,1)} %get-tuple-element.10.main_ref) | copy-start | bytes 3145732
  98.6 21.6 %all-to-all-start.1 = ((bf16[64,8,640]{2,1,0:T(8,128)(2,1)}), bf16[64,8,640]{2,1,0:T(8,128)(2,1)S(1)}, u32[]{:S(2)}, u32[]{:S(2)}) async-start(bf16[64,8,640]{2,1,0:T(8,128)(2,1)} %broadcast_in_dim.27), calls=%async_computation.1 | async-start | bytes 1310720 | tf_op jit(solution)/shard_map/all_to_all | solution.py:399
  103.3 6.3 %collective-permute-start.5 = (bf16[16,3,256]{2,1,0:T(4,128)(2,1)S(1)}, bf16[16,3,256]{2,1,0:T(4,128)(2,1)S(1)}, u32[]{:S(2)}, u32[]{:S(2)}) collective-permute-start(bf16[16,3,256]{2,1,0:T(4,128)(2,1)S(1)} %get-tuple-element.34), channel_id=1, source_target_pairs={{0,120},{8,0},{16,8},{24,16},{32,24},{40,32},{48,40},{56,48},{64,5... | collective-permute-start | bytes 73736 | tf_op jit(solution)/shard_map/ppermute | solution.py:298
  107.9 7.9 %collective-permute-start.4 = (bf16[16,3,256]{2,1,0:T(4,128)(2,1)S(1)}, bf16[16,3,256]{2,1,0:T(4,128)(2,1)S(1)}, u32[]{:S(2)}, u32[]{:S(2)}) collective-permute-start(bf16[16,3,256]{2,1,0:T(4,128)(2,1)S(1)} %get-tuple-element.35), channel_id=1, source_target_pairs={{0,8},{8,16},{16,24},{24,32},{32,40},{40,48},{48,56},{56,64},{64,7... | collective-permute-start | bytes 73736 | tf_op jit(solution)/shard_map/ppermute | solution.py:297
  116.2 6.2 %collective-permute-start.7 = (bf16[3,144,256]{2,1,0:T(8,128)(2,1)S(1)}, bf16[3,144,256]{2,1,0:T(8,128)(2,1)S(1)}, u32[]{:S(2)}, u32[]{:S(2)}) collective-permute-start(bf16[3,144,256]{2,1,0:T(8,128)(2,1)S(1)} %get-tuple-element.30), channel_id=1, source_target_pairs={{0,7},{1,0},{2,1},{3,2},{4,3},{5,4},{6,5},{7,6},{8,15},{9,8},{10,9... | collective-permute-start | bytes 663560 | tf_op jit(solution)/shard_map/ppermute | solution.py:306
  118.9 8.0 %collective-permute-start.6 = (bf16[3,144,256]{2,1,0:T(8,128)(2,1)S(1)}, bf16[3,144,256]{2,1,0:T(8,128)(2,1)S(1)}, u32[]{:S(2)}, u32[]{:S(2)}) collective-permute-start(bf16[3,144,256]{2,1,0:T(8,128)(2,1)S(1)} %get-tuple-element.31), channel_id=1, source_target_pairs={{0,1},{1,2},{2,3},{3,4},{4,5},{5,6},{6,7},{7,0},{8,9},{9,10},{10,1... | collective-permute-start | bytes 663560 | tf_op jit(solution)/shard_map/ppermute | solution.py:305
  120.2 21.9 %collective-permute-start.8 = (bf16[64,8,640]{2,1,0:T(8,128)(2,1)S(1)}, bf16[64,8,640]{2,1,0:T(8,128)(2,1)S(1)}, u32[]{:S(2)}, u32[]{:S(2)}) collective-permute-start(bf16[64,8,640]{2,1,0:T(8,128)(2,1)S(1)} %all-to-all-done.1), channel_id=1, source_target_pairs={{0,8},{8,0},{1,9},{9,1},{2,10},{10,2},{3,11},{11,3},{4,12},{12,4},... | collective-permute-start | bytes 1966088 | tf_op jit(solution)/shard_map/ppermute | solution.py:402
  122.4 4.6 %copy-start.5 = (bf16[3,144,256]{2,1,0:T(8,128)(2,1)}, bf16[3,144,256]{2,1,0:T(8,128)(2,1)S(1)}, u32[]{:S(2)}) copy-start(bf16[3,144,256]{2,1,0:T(8,128)(2,1)S(1)} %collective-permute-done.7.north_ref) | copy-start | bytes 663556
  127.0 0.7 copy-start.6

commit v2 on v1

v2 whole, which is shorter than its diff:
```python
import functools
import math

import jax
import jax.numpy as jnp
from jax import lax
from jax.experimental import pallas as pl
from jax.experimental.pallas import tpu as pltpu
from jax.sharding import Mesh
from jax.sharding import PartitionSpec as P

KS = 7
MARGIN = KS // 2
HALF = 128
STEP = 8
SPAN = 16
EDGE = 8
SLOTS = 64
FORWARD_VMEM = 56 * 1024 * 1024
BACKWARD_VMEM = 28 * 1024 * 1024
GROUP = 4
CUTS = ((0, 2), (2, 4), (4, 7))
TAPS = (KS + 1) // 2 * KS
GELU_SCALE = math.sqrt(2.0 / math.pi)
GELU_CUBE = 0.044715
EPSILON = 1e-06
LON = ("x", "zh", "core")
LAT = ("zl", "y")
CHIPS = ("x", "zh", "zl", "y")
ALL = ("x", "zh", "core", "zl", "y")
F32 = jnp.float32
BF16 = jnp.bfloat16


def dot(a, b):
    return jnp.dot(a, b, preferred_element_type=F32)


def build_weights(taps_ref, w_ref, flip):
    rows = lax.broadcasted_iota(jnp.int32, (HALF, HALF), 0)
    cols = lax.broadcasted_iota(jnp.int32, (HALF, HALF), 1)
    eye = rows == cols
    zero = jnp.zeros((HALF, HALF), F32)
    for h in range(2):
        for i2 in range((KS + 1) // 2):
            for j in range(KS):
                tile = i2 * KS + j
                for a in range(2):
                    for b in range(2):
                        i = 2 * i2 + a - b
                        if 0 <= i < KS:
                            tap = (KS - 1 - i) * KS + (KS - 1 - j) if flip else i * KS + j
                            row = taps_ref[tap // KS, tap % KS : tap % KS + 1, h * HALF : (h + 1) * HALF]
                            block = jnp.where(eye, row, zero)
                        else:
                            block = zero
                        w_ref[
                            h,
                            tile * 256 + a * HALF : tile * 256 + (a + 1) * HALF,
                            b * HALF : (b + 1) * HALF,
                        ] = block.astype(BF16)


def assemble(main_ref, near_ref, far_ref, south_ref, north_ref, wide, xs):
    rows, tile, _ = main_ref.shape
    even = lax.axis_index("core") == 0
    band = lax.axis_index(LAT)
    below = jnp.where(band > 0, 1.0, 0.0).astype(F32)
    above = jnp.where(band < lax.axis_size(LAT) - 1, 1.0, 0.0).astype(F32)
    for h in range(2):
        lanes = slice(h * HALF, (h + 1) * HALF)
        wide[h, 0:MARGIN] = south_ref[:, :, lanes].astype(F32) * below
        wide[h, rows + MARGIN : rows + 2 * MARGIN] = north_ref[:, :, lanes].astype(F32) * above

    def place(pair, _):
        for r in (2 * pair, 2 * pair + 1):
            for h in range(2):
                lanes = slice(h * HALF, (h + 1) * HALF)
                wide[h, r + MARGIN, EDGE : EDGE + tile, :] = main_ref[r, :, lanes].astype(F32)
                near = near_ref[r, :, lanes].astype(F32)
                far = far_ref[r, :, lanes].astype(F32)
                wide[h, r + MARGIN, 0:EDGE, :] = jnp.where(even, far, near)
                wide[h, r + MARGIN, EDGE + tile : 2 * EDGE + tile, :] = jnp.where(even, near, far)
        return 0

    lax.fori_loop(0, rows // 2, place, 0)

    def spread(pair, _):
        for r in (2 * pair, 2 * pair + 1):
            for h in range(2):
                for t in range(STEP + 2 * MARGIN):
                    piece = wide[h, r, pl.ds(EDGE - MARGIN + t, SPAN, stride=STEP), :]
                    xs[h, r, t] = piece.astype(BF16)
        return 0

    lax.fori_loop(0, rows // 2 + MARGIN, spread, 0)


def stage_cotangent(cot_ref, sea_ref, slot_ref, slots, cot_wide, mask_wide):
    rows, tile, _ = cot_ref.shape
    open_cells = (sea_ref[...] > 0) & (slot_ref[...] < slots)
    mask = jnp.where(open_cells, 1.0, 0.0).astype(F32)
    mask = jnp.concatenate([mask, jnp.zeros((HALF - rows, tile), F32)], axis=0).T
    for r in range(rows):
        column = jnp.broadcast_to(mask[:, r : r + 1], (tile, HALF))
        mask_wide[r] = column
        for h in range(2):
            cot_wide[h, r] = cot_ref[r, :, h * HALF : (h + 1) * HALF].astype(F32) * column


def conv_part(xs, w_ref, h, pair, i2, first, last):
    pieces = []
    for j in range(first, last):
        for a in range(2):
            pieces.append(xs[h, 2 * pair + 2 * i2 + a, j : j + STEP].reshape(STEP * SPAN, HALF))
    span = slice((i2 * KS + first) * 256, (i2 * KS + last) * 256)
    return dot(jnp.concatenate(pieces, axis=1), w_ref[h, span])


def conv_pair(xs, w_ref, h, pair):
    total = conv_part(xs, w_ref, h, pair, 0, 0, KS)
    for i2 in range(1, (KS + 1) // 2):
        total = total + conv_part(xs, w_ref, h, pair, i2, 0, KS)
    return total


def conv_group(xs, w_ref, h, pair):
    pieces = []
    for i2 in range((KS + 1) // 2):
        for j in range(KS):
            for a in range(2):
                rows = [2 * (pair + n) + 2 * i2 + a for n in range(GROUP)]
                pieces.append(
                    jnp.concatenate(
                        [xs[h, r, j : j + STEP].reshape(STEP * SPAN, HALF) for r in rows], axis=0
                    )
                )
    return dot(jnp.concatenate(pieces, axis=1), w_ref[h])


def tap_part(gm_xs, wide, h, i, b, side, pair, sums):
    source = jnp.maximum(pair, 0)
    part = slice(side * 8, side * 8 + 8)
    grads = [gm_xs[h, 2 * pair + 2 + b, t, part] for t in range(STEP)]
    for spot in range(STEP + KS - 1):
        cell = wide[
            h,
            2 * source + b + i,
            pl.ds(EDGE - MARGIN + spot + side * 8 * STEP, 8, stride=STEP),
            :,
        ]
        for j in range(KS):
            if 0 <= spot - j < STEP:
                sums[j] = sums[j] + grads[spot - j] * cell
    return sums


def add_taps(gm_xs, wide, acc_taps, h, i, pair):
    sums = [acc_taps[h, i * KS + j] for j in range(KS)]
    for b in range(2):
        for side in range(2):
            sums = tap_part(gm_xs, wide, h, i, b, side, pair, sums)
    for j in range(KS):
        acc_taps[h, i * KS + j] = sums[j]


def zipped(*lists):
    spots = [((k + 0.5) / len(items), n, k) for n, items in enumerate(lists) for k in range(len(items))]
    return [lists[n][k] for _, n, k in sorted(spots)]


def strided(ref, row):
    return jnp.concatenate(
        [ref[row, pl.ds(t, SPAN, stride=STEP), :] for t in range(STEP)], axis=0
    )


def pack_sums(targets, acc_in, acc_out, acc_scale, acc_taps):
    half_ff = acc_in.shape[1] // 2
    spots = targets[0].shape[0]

    def pack(quad, _):
        for g in range(4):
            group = 4 * quad + g
            for target, acc in zip(targets, (acc_in, acc_out)):
                for side in range(2):
                    target[group * 2 + side, :, 0:half_ff] = acc[
                        pl.ds(pl.multiple_of(group * 8, 8), 8),
                        side * half_ff : (side + 1) * half_ff,
                    ].astype(BF16)
        return 0

    lax.fori_loop(0, spots // 8, pack, 0)
    for spot in range(2 * spots):
        tap, h = spot // 2, spot % 2
        if tap < KS * KS:
            value = acc_taps[h, tap]
        elif tap == KS * KS:
            value = acc_scale[:, h * HALF : (h + 1) * HALF]
        else:
            value = jnp.zeros((8, HALF), F32)
        targets[spot // spots][spot % spots, :, half_ff:] = value.astype(BF16)


def forward_kernel(
    main_ref,
    near_ref,
    far_ref,
    south_ref,
    north_ref,
    cot_ref,
    sea_ref,
    slot_ref,
    taps_ref,
    gain_ref,
    bias_ref,
    w_in_ref,
    w_in_t_ref,
    b_in_ref,
    w_out_ref,
    w_out_t_ref,
    scale_ref,
    out_ref,
    gm_ref,
    keep_ref,
    send_ref,
    wide,
    xs,
    w_ref,
    out_wide,
    gm_wide,
    gm_xs,
    mask_wide,
    mixed_ref,
    acc_taps,
    acc_in,
    acc_out,
    acc_scale,
):
    rows = main_ref.shape[0]
    ff = w_in_ref.shape[1]
    width = 2 * HALF
    cells = 2 * STEP * SPAN
    build_weights(taps_ref, w_ref, False)
    assemble(main_ref, near_ref, far_ref, south_ref, north_ref, wide, xs)
    stage_cotangent(cot_ref, sea_ref, slot_ref, SLOTS, out_wide, mask_wide)
    acc_in[...] = jnp.zeros_like(acc_in)
    acc_out[...] = jnp.zeros_like(acc_out)
    acc_scale[...] = jnp.zeros_like(acc_scale)
    gain, bias, scale = gain_ref[...], bias_ref[...], scale_ref[...]

    acc_taps[...] = jnp.zeros_like(acc_taps)
    for h in range(2):
        gm_xs[h, 0:2] = jnp.zeros((2, STEP, SPAN, HALF), F32)
        mixed_ref[h] = conv_pair(xs, w_ref, h, 0)

    def finish(pair):
        for row in (2 * pair, 2 * pair + 1):
            for h in range(2):
                lanes = slice(h * HALF, (h + 1) * HALF)
                out_ref[row, :, lanes] = out_wide[h, row].astype(BF16)
                gm_ref[row, :, lanes] = gm_wide[h, row].astype(BF16)

    def pair_step(pair, _):
        finish(jnp.maximum(pair - 1, 0))
        low, high = mixed_ref[0], mixed_ref[1]
        mixed = jnp.concatenate(
            [
                jnp.concatenate([low[:, :HALF], high[:, :HALF]], axis=1),
                jnp.concatenate([low[:, HALF:], high[:, HALF:]], axis=1),
            ],
            axis=0,
        )
        later = jnp.minimum(pair + 1, rows // 2 - 1)
        conv_tasks, tap_tasks = [], []
        for h in range(2):
            begun = {}

            def conv_task(h, i2, first, last, begun):
                part = conv_part(xs, w_ref, h, later, i2, first, last)
                begun[0] = part if 0 not in begun else begun[0] + part
                if i2 == (KS - 1) // 2 and last == KS:
                    mixed_ref[h] = begun[0]

            for i2 in range((KS + 1) // 2):
                for first, last in CUTS:
                    conv_tasks.append(functools.partial(conv_task, h, i2, first, last, begun))
            for i in range(KS):
                tap_tasks.append(
                    functools.partial(add_taps, gm_xs, wide, acc_taps, h, i, pair - 1)
                )
        for work in zipped(conv_tasks, tap_tasks):
            work()
        mean = jnp.mean(mixed, axis=1, keepdims=True)
        centered = mixed - mean
        var = jnp.mean(centered * centered, axis=1, keepdims=True)
        inverse = lax.rsqrt(var + EPSILON)
        normed = centered * inverse
        normalized = (normed * gain + bias).astype(BF16)
        cot = jnp.concatenate(
            [
                jnp.concatenate([strided(out_wide.at[h], 2 * pair + b) for b in range(2)], axis=0)
                for h in range(2)
            ],
            axis=1,
        )
        grad_out = (cot * scale).astype(BF16)
        branch = jnp.zeros((cells, width), F32)
        grad_norm = jnp.zeros((cells, width), F32)
        normalized_t = normalized.T
        grad_out_t = grad_out.T
        parts = ff // 256
        def enter(f):
            part = slice(f * 256, (f + 1) * 256)
            return (
                dot(normalized, w_in_ref[:, part]) + b_in_ref[:, part],
                dot(grad_out, w_out_t_ref[:, part]),
            )

        ahead = enter(0)
        for f in range(parts):
            part = slice(f * 256, (f + 1) * 256)
            hidden, grad_act = ahead
            if f + 1 < parts:
                ahead = enter(f + 1)
            square = hidden * hidden
            hyper = jnp.tanh(hidden * (GELU_SCALE + GELU_SCALE * GELU_CUBE * square))
            gate = 0.5 + 0.5 * hyper
            act = hidden * gate
            slope = gate + act * (1.0 - gate) * (
                2.0 * GELU_SCALE + 6.0 * GELU_SCALE * GELU_CUBE * square
            )
            act_low = act.astype(BF16)
            grad_hidden = (grad_act * slope).astype(BF16)
            branch = branch + dot(act_low, w_out_ref[part, :])
            grad_norm = grad_norm + dot(grad_hidden, w_in_t_ref[part, :])
            acc_in[:, part] += dot(normalized_t, grad_hidden)
            acc_out[:, part] += dot(grad_out_t, act_low)
        branch = branch.astype(BF16).astype(F32)
        acc_scale[...] += jnp.sum((cot * branch).reshape(cells // 8, 8, width), axis=0)
        g = grad_norm.astype(BF16).astype(F32) * gain
        grad_mixed = inverse * (
            g
            - jnp.mean(g, axis=1, keepdims=True)
            - normed * jnp.mean(g * normed, axis=1, keepdims=True)
        )
        grad_mixed = grad_mixed.astype(BF16).astype(F32)
        mask = jnp.concatenate([strided(mask_wide, 2 * pair + b) for b in range(2)], axis=0)
        for h in range(2):
            lanes = slice(h * HALF, (h + 1) * HALF)
            added = mask * scale[:, lanes] * branch[:, lanes]
            for b in range(2):
                row = 2 * pair + b
                for t in range(STEP):
                    start = b * STEP * SPAN + t * SPAN
                    feature = wide[h, row + MARGIN, pl.ds(EDGE + t, SPAN, stride=STEP), :]
                    out_wide[h, row, pl.ds(t, SPAN, stride=STEP), :] = (
                        feature + added[start : start + SPAN]
                    )
                    piece = grad_mixed[start : start + SPAN, lanes]
                    gm_wide[h, row, pl.ds(t, SPAN, stride=STEP), :] = piece
                    gm_xs[h, row + 2, t] = piece
        return 0

    lax.fori_loop(0, rows // 2, pair_step, 0)

    finish(rows // 2 - 1)
    for h in range(2):
        for i in range(KS):
            add_taps(gm_xs, wide, acc_taps, h, i, rows // 2 - 1)
    core = lax.axis_index("core")

    @pl.when(core == 0)
    def _():
        pack_sums((keep_ref, send_ref), acc_in, acc_out, acc_scale, acc_taps)

    @pl.when(core != 0)
    def _():
        pack_sums((send_ref, keep_ref), acc_in, acc_out, acc_scale, acc_taps)


def backward_kernel(
    main_ref,
    near_ref,
    far_ref,
    south_ref,
    north_ref,
    cot_ref,
    taps_ref,
    out_ref,
    wide,
    xs,
    w_ref,
    out_wide,
):
    rows = main_ref.shape[0]
    build_weights(taps_ref, w_ref, True)
    assemble(main_ref, near_ref, far_ref, south_ref, north_ref, wide, xs)

    def finish(group, h):
        lanes = slice(h * HALF, (h + 1) * HALF)
        for b in range(2 * GROUP):
            row = 2 * GROUP * group + b
            out_ref[row, :, lanes] = (
                cot_ref[row, :, lanes].astype(F32) + out_wide[h, row]
            ).astype(BF16)

    def group_step(group, _):
        for h in range(2):
            both = conv_group(xs, w_ref, h, GROUP * group)
            for n in range(GROUP):
                for b in range(2):
                    for t in range(STEP):
                        start = (n * STEP + t) * SPAN
                        row = 2 * (GROUP * group + n) + b
                        out_wide[h, row, pl.ds(t, SPAN, stride=STEP), :] = both[
                            start : start + SPAN, b * HALF : (b + 1) * HALF
                        ]
            finish(group, h)
        return 0

    lax.fori_loop(0, rows // 2 // GROUP, group_step, 0)


def rim_sides(field):
    tile = field.shape[1]
    even = lax.axis_index("core") == 0
    low, high = field[:, :EDGE], field[:, tile - EDGE :]
    count = lax.axis_size(LON)
    across = [(i, (i + 1) % count) for i in range(1, count, 2)]
    across += [(target, source) for source, target in across]
    far = lax.ppermute(jnp.where(even, low, high), LON, across)
    near = lax.ppermute(jnp.where(even, high, low), "core", [(0, 1), (1, 0)])
    return near, far


def rim_messages(field, near, far):
    rows = field.shape[0]
    even = lax.axis_index("core") == 0

    def across(part):
        west = jnp.where(even, far[part], near[part])
        east = jnp.where(even, near[part], far[part])
        return jnp.concatenate([west, field[part], east], axis=1)

    return across(slice(rows - MARGIN, rows)), across(slice(0, MARGIN))


def rim_ends(up, down):
    count = lax.axis_size(LAT)
    forward = [(i, (i + 1) % count) for i in range(count)]
    backward = [(i, (i - 1) % count) for i in range(count)]
    return lax.ppermute(up, LAT, forward), lax.ppermute(down, LAT, backward)


def on_device(
    features, cotangent, land_sea, tile_slot, kernel, ln_gain, ln_bias, w_in, b_in, w_out, layer_scale
):
    rows, tile, width = features.shape
    ff = w_in.shape[1]
    chips = lax.axis_size(CHIPS)
    padded = rows + 2 * MARGIN
    ext = STEP + 2 * MARGIN
    vmem = pl.BlockSpec(memory_space=pltpu.VMEM)
    wide = pltpu.VMEM((2, padded, tile + 2 * EDGE, HALF), F32)
    xs = pltpu.VMEM((2, padded, ext, SPAN, HALF), BF16)
    weights = pltpu.VMEM((2, TAPS * 256, 256), BF16)
    flat = pltpu.VMEM((2, rows, tile, HALF), F32)
    near, far = rim_sides(features)
    south, north = rim_ends(*rim_messages(features, near, far))
    chunk = ff // 2 + HALF
    output, grad_mixed, keep, send = pl.pallas_call(
        forward_kernel,
        out_shape=(
            jax.ShapeDtypeStruct(features.shape, BF16),
            jax.ShapeDtypeStruct(features.shape, BF16),
            jax.ShapeDtypeStruct((chips, 8, chunk), BF16),
            jax.ShapeDtypeStruct((chips, 8, chunk), BF16),
        ),
        in_specs=[vmem] * 17,
        out_specs=(vmem,) * 4,
        scratch_shapes=[
            wide,
            xs,
            weights,
            flat,
            flat,
            pltpu.VMEM((2, rows + 2, STEP, SPAN, HALF), F32),
            pltpu.VMEM((rows, tile, HALF), F32),
            pltpu.VMEM((2, STEP * SPAN, 256), F32),
            pltpu.VMEM((2, KS * KS, 8, HALF), F32),
            pltpu.VMEM((width, ff), F32),
            pltpu.VMEM((width, ff), F32),
            pltpu.VMEM((8, width), F32),
        ],
        compiler_params=pltpu.CompilerParams(vmem_limit_bytes=FORWARD_VMEM),
        cost_estimate=pl.CostEstimate(
            flops=14_000_000_000, bytes_accessed=8_000_000, transcendentals=2_000_000
        ),
        name="forward",
    )(
        features,
        near,
        far,
        south,
        north,
        cotangent,
        land_sea,
        tile_slot,
        kernel,
        ln_gain.reshape(1, width),
        ln_bias.reshape(1, width),
        w_in,
        w_in.T,
        b_in.reshape(1, ff),
        w_out,
        w_out.T,
        layer_scale.reshape(1, width),
    )
    swap = [(0, 1), (1, 0)]
    near, far = rim_sides(grad_mixed)
    sums = (keep.astype(F32) + lax.ppermute(send, "core", swap).astype(F32)).astype(BF16)
    south, north = rim_ends(*rim_messages(grad_mixed, near, far))
    arrived = lax.all_to_all(sums, CHIPS, split_axis=0, concat_axis=0, tiled=True)
    own, grad_mixed, near, far, south, north = lax.optimization_barrier(
        (
            jnp.sum(arrived.astype(F32), axis=0).astype(BF16),
            grad_mixed,
            near,
            far,
            south,
            north,
        )
    )
    mine = lax.all_to_all(
        jnp.broadcast_to(own[None], (chips,) + own.shape), CHIPS, split_axis=0, concat_axis=0, tiled=True
    )
    grad_features = pl.pallas_call(
        backward_kernel,
        out_shape=jax.ShapeDtypeStruct(features.shape, BF16),
        in_specs=[vmem] * 7,
        out_specs=vmem,
        scratch_shapes=[wide, xs, weights, flat],
        compiler_params=pltpu.CompilerParams(vmem_limit_bytes=BACKWARD_VMEM),
        cost_estimate=pl.CostEstimate(
            flops=7_000_000_000, bytes_accessed=4_000_000, transcendentals=0
        ),
        name="backward",
    )(grad_mixed, near, far, south, north, cotangent, kernel)
    mine, grad_features = lax.optimization_barrier((mine, grad_features))
    other = lax.ppermute(mine, "core", swap)
    first = lax.axis_index("core") == 0
    whole = jnp.stack([jnp.where(first, mine, other), jnp.where(first, other, mine)])
    factor = 1.0 / math.sqrt(rows * lax.axis_size(LAT) * tile * lax.axis_size(LON))
    main = whole[..., : ff // 2].reshape(2, width // 8, 2, 8, ff // 2)
    main = main.transpose(0, 1, 3, 2, 4).reshape(2, width, ff).astype(F32) * factor
    small = whole[..., ff // 2 :].reshape(2 * chips, 8, HALF)[: 2 * (KS * KS + 1)]
    small = jnp.sum(small.astype(F32), axis=1) * factor
    small = small.reshape(KS * KS + 1, width)
    return (
        output,
        grad_features,
        main[0],
        main[1].T,
        small[: KS * KS].reshape(KS, KS, width),
        small[KS * KS],
    )


def solution(mesh):
    fine = Mesh(mesh.devices.reshape(4, 2, 2, 2, 4), ("x", "zh", "core", "zl", "y"))
    cells = P(LAT, LON, None)
    return jax.shard_map(
        on_device,
        mesh=fine,
        in_specs=(cells, cells, P(LAT, LON), P(LAT, LON)) + (P(),) * 7,
        out_specs=(cells, cells, P(), P(), P(), P()),
        check_vma=False,
    )
```

time: 147 us -> 118 us (0.80)
  blocking collectives: 28 us -> 0 us
  starting transfers between devices: 21.1 us -> 33.6 us
  local copies, waits for them, and re-layouts: 19.8 us -> 10.8 us
  Pallas kernels: 52.3 us -> 47.1 us
  waiting for transfers between devices: 19.8 us -> 18.3 us
    all_to_all x1 -> x0, blocking collectives: 28 us -> none  [on_device(): arrived = lax.all_to_all(sums, ALL, split_axis=0, concat_axis=0, tiled=True)]
    ppermute x9 -> x10, waiting for transfers between devices: 19.8 us -> 5.5 us  [the longest x4 2.5 us: rim_ends(): return (lax.ppermute(up, LAT, forward), lax.ppermute(down, LAT, backward))]
    all_to_all x0 -> x1, waiting for transfers between devices: none -> 9.55 us  [on_device(): lax.all_to_all(sums, CHIPS, split_axis=0, concat_axis=0, tiled=True)]
    all_to_all x0 -> x1, starting transfers between devices: none -> 7.09 us  [on_device(): lax.all_to_all(sums, CHIPS, split_axis=0, concat_axis=0, tiled=True)]
    concatenate x6 -> x0, local copies, waits for them, and re-layouts: 6.87 us -> none  [the longest x2 4.3 us: rim(): full = jnp.concatenate([west, field, east], axis=1)]
    all_to_all x1, waiting for transfers between devices: 0.01 us -> 3.27 us  [on_device(): lax.all_to_all(jnp.broadcast_to(own[None], (chips,) + own.shape), CHIPS,...]
    pallas_call x1, Pallas kernels: 14.4 us -> 11.3 us  [on_device(): pl.pallas_call(backward_kernel, out_shape=jax.ShapeDtypeStruct(features.s...]
    all_to_all x1, starting transfers between devices: 4.64 us -> 7.67 us  [on_device(): lax.all_to_all(jnp.broadcast_to(own[None], (chips,) + own.shape), CHIPS,...]
  transfers between devices with their start and end apart: 10 -> 12, of which waited for: 6 -> 6; matrix products, arithmetic and copies ran while one was open for 8% -> 9% of each run, Pallas kernels for 10% -> 10%
where the time goes in v2:
time: 118 us; the launch traced here: 117 us
  Pallas kernels  47.1 us (40%)
  starting transfers between devices  33.6 us (28%)
  waiting for transfers between devices  18.3 us (16%)
  local copies, waits for them, and re-layouts  10.8 us (9%)
  other arithmetic  6.07 us (5%)
    pallas_call x1, Pallas kernels, on_device(): pl.pallas_call(forward_kernel, out_shape=(jax.ShapeDtypeStruct(features.s...  35.8 us
    pallas_call x1, Pallas kernels, on_device(): pl.pallas_call(backward_kernel, out_shape=jax.ShapeDtypeStruct(features.s...  11.3 us
    ppermute x2, starting transfers between devices, rim_sides(): far = lax.ppermute(jnp.where(even, low, high), LON, across)  10.3 us
    all_to_all x1, waiting for transfers between devices, on_device(): lax.all_to_all(sums, CHIPS, split_axis=0, concat_axis=0, tiled=True)  9.55 us
    ppermute x4, starting transfers between devices, rim_ends(): return (lax.ppermute(up, LAT, forward), lax.ppermute(down, LAT, backward))  8.5 us
    all_to_all x1, starting transfers between devices, on_device(): lax.all_to_all(jnp.broadcast_to(own[None], (chips,) + own.shape), CHIPS,...  7.67 us
    all_to_all x1, starting transfers between devices, on_device(): lax.all_to_all(sums, CHIPS, split_axis=0, concat_axis=0, tiled=True)  7.09 us
    unnamed x22, local copies, waits for them, and re-layouts  5.44 us
  transfers between devices with their start and end apart: 12, of which 6 were waited for; matrix products, arithmetic and copies ran while one was open for 9% of the time, Pallas kernels for 10%

profile of v2, /device:TPU:0, one launch (start us, length us, event | category | flops | bytes accessed | tf_op | source)
XLA Modules:
  0.0 116.7 jit_solution(13083934875948422154)
XLA Ops:
  0.7 1.0 broadcast_select_fusion.2
  1.6 5.7 %collective-permute-start.1 = (bf16[16,8,256]{2,1,0:T(8,128)(2,1)S(1)}, bf16[16,8,256]{2,1,0:T(8,128)(2,1)S(1)}, u32[]{:S(2)}, u32[]{:S(2)}) collective-permute-start(bf16[16,8,256]{2,1,0:T(8,128)(2,1)S(1)} %get-tuple-element.46), channel_id=1, source_target_pairs={{8,16},{24,32},{40,48},{56,64},{72,80},{88,96},{104,112},{120,0},{... | collective-permute-start | bytes 196616 | tf_op jit(solution)/shard_map/ppermute | solution.py:432
  7.3 1.0 fusion.3
  8.4 0.9 collective-permute-done.1.far_ref
  9.3 1.6 %collective-permute-start.2 = (bf16[3,144,256]{2,1,0:T(8,128)(2,1)S(1)}, bf16[3,144,256]{2,1,0:T(8,128)(2,1)S(1)}, u32[]{:S(2)}, u32[]{:S(2)}) collective-permute-start(bf16[3,144,256]{2,1,0:T(8,128)(2,1)S(1)} %pad_maximum_fusion.1), channel_id=1, source_target_pairs={{0,1},{1,2},{2,3},{3,4},{4,5},{5,6},{6,7},{7,0},{8,9},{9,10},{10,1... | collective-permute-start | bytes 663560 | tf_op jit(solution)/shard_map/ppermute | solution.py:453
  11.0 2.7 %collective-permute-start.3 = (bf16[3,144,256]{2,1,0:T(8,128)(2,1)S(1)}, bf16[3,144,256]{2,1,0:T(8,128)(2,1)S(1)}, u32[]{:S(2)}, u32[]{:S(2)}) collective-permute-start(bf16[3,144,256]{2,1,0:T(8,128)(2,1)S(1)} %pad_maximum_fusion.2), channel_id=1, source_target_pairs={{0,7},{1,0},{2,1},{3,2},{4,3},{5,4},{6,5},{7,6},{8,15},{9,8},{10,9... | collective-permute-start | bytes 663560 | tf_op jit(solution)/shard_map/ppermute | solution.py:453
  13.7 1.3 %copy.23.slot_ref = s32[16,1]{1,0:T(8,128)} copy(s32[16,1]{0,1:T(1,128)} %param.14) | data formatting | bytes 128 | tf_op args[3]
  15.0 1.0 copy.21
  16.0 1.0 copy.22
  17.0 1.4 %collective-permute-done.2.south_ref = bf16[3,144,256]{2,1,0:T(8,128)(2,1)S(1)} collective-permute-done((bf16[3,144,256]{2,1,0:T(8,128)(2,1)S(1)}, bf16[3,144,256]{2,1,0:T(8,128)(2,1)S(1)}, u32[]{:S(2)}, u32[]{:S(2)}) %collective-permute-start.2) | collective-permute-done | bytes 221216 | tf_op jit(solution)/shard_map/ppermute | solution.py:453
  18.5 0.7 copy-done.7
  19.2 35.8 %forward.1 = (bf16[16,128,256]{2,1,0:T(8,128)(2,1)}, bf16[16,128,256]{2,1,0:T(8,128)(2,1)}, bf16[64,8,640]{2,1,0:T(8,128)(2,1)}, bf16[64,8,640]{2,1,0:T(8,128)(2,1)}) custom-call(bf16[16,128,256]{2,1,0:T(8,128)(2,1)} %main_ref.1, bf16[16,8,256]{2,1,0:T(8,128)(2,1)} %copy-done.6, bf16[16,8,256]{2,1,0:T(8,128)(2,1)} %copy-done.5, ...), custom_call_target="tpu_custom_call" | custom-call | flops 14000000000 | bytes 8000000 | tf_op jit(solution)/shard_map/forward/pallas_call | solution.py:472
  55.0 0.9 broadcast_select_fusion
  55.9 4.6 %collective-permute-start.6 = (bf16[16,8,256]{2,1,0:T(8,128)(2,1)S(1)}, bf16[16,8,256]{2,1,0:T(8,128)(2,1)S(1)}, u32[]{:S(2)}, u32[]{:S(2)}) collective-permute-start(bf16[16,8,256]{2,1,0:T(8,128)(2,1)S(1)} %get-tuple-element.42), channel_id=1, source_target_pairs={{8,16},{24,32},{40,48},{56,64},{72,80},{88,96},{104,112},{120,0},{... | collective-permute-start | bytes 196616 | tf_op jit(solution)/shard_map/ppermute | solution.py:432
  60.6 1.0 fusion.2
  61.6 2.1 %add_convert_fusion = bf16[64,8,640]{2,1,0:T(8,128)(2,1)} fusion(bf16[64,8,640]{2,1,0:T(8,128)(2,1)S(1)} %collective-permute-done.4, bf16[64,8,640]{2,1,0:T(8,128)(2,1)} %get-tuple-element.19), kind=kLoop, calls=%fused_computation.3 | loop fusion | flops 1310720 | bytes 1966080 | tf_op jit(solution)/shard_map/convert_element_type | solution.py:522
  63.7 7.1 %all-to-all-start = ((bf16[64,8,640]{2,1,0:T(8,128)(2,1)}), bf16[64,8,640]{2,1,0:T(8,128)(2,1)S(1)}, u32[]{:S(2)}, u32[]{:S(2)}) async-start(bf16[64,8,640]{2,1,0:T(8,128)(2,1)} %add_convert_fusion), calls=%async_computation | async-start | bytes 1310720 | tf_op jit(solution)/shard_map/all_to_all | solution.py:524
  70.9 0.7 pad_maximum_fusion.3
  71.6 1.6 %collective-permute-start.7 = (bf16[3,144,256]{2,1,0:T(8,128)(2,1)}, bf16[3,144,256]{2,1,0:T(8,128)(2,1)S(1)}, u32[]{:S(2)}, u32[]{:S(2)}) collective-permute-start(bf16[3,144,256]{2,1,0:T(8,128)(2,1)} %pad_maximum_fusion.3), channel_id=1, source_target_pairs={{0,1},{1,2},{2,3},{3,4},{4,5},{5,6},{6,7},{7,0},{8,9},{9,10},{10,1... | collective-permute-start | bytes 663560 | tf_op jit(solution)/shard_map/ppermute | solution.py:453
  73.2 0.7 pad_maximum_fusion.4
  73.8 2.6 %collective-permute-start.8 = (bf16[3,144,256]{2,1,0:T(8,128)(2,1)}, bf16[3,144,256]{2,1,0:T(8,128)(2,1)S(1)}, u32[]{:S(2)}, u32[]{:S(2)}) collective-permute-start(bf16[3,144,256]{2,1,0:T(8,128)(2,1)} %pad_maximum_fusion.4), channel_id=1, source_target_pairs={{0,7},{1,0},{2,1},{3,2},{4,3},{5,4},{6,5},{7,6},{8,15},{9,8},{10,9... | collective-permute-start | bytes 663560 | tf_op jit(solution)/shard_map/ppermute | solution.py:453
  76.4 9.6 %all-to-all-done = bf16[64,8,640]{2,1,0:T(8,128)(2,1)S(1)} async-done(((bf16[64,8,640]{2,1,0:T(8,128)(2,1)}), bf16[64,8,640]{2,1,0:T(8,128)(2,1)S(1)}, u32[]{:S(2)}, u32[]{:S(2)}) %all-to-all-start) | async-done | bytes 655392 | tf_op jit(solution)/shard_map/all_to_all | solution.py:524
  86.1 1.1 collective-permute-done.7.south_ref
  87.2 0.9 broadcast_in_dim.2
  88.1 7.7 %all-to-all-start.1 = ((bf16[64,8,640]{2,1,0:T(8,128)(2,1)}), bf16[64,8,640]{2,1,0:T(8,128)(2,1)S(1)}, u32[]{:S(2)}, u32[]{:S(2)}) async-start(bf16[64,8,640]{2,1,0:T(8,128)(2,1)} %broadcast_in_dim.2), calls=%async_computation.1 | async-start | bytes 1310720 | tf_op jit(solution)/shard_map/all_to_all | solution.py:535
  95.8 11.3 %backward.1 = bf16[16,128,256]{2,1,0:T(8,128)(2,1)} custom-call(bf16[16,128,256]{2,1,0:T(8,128)(2,1)S(1)} %copy-done, bf16[16,8,256]{2,1,0:T(8,128)(2,1)S(1)} %collective-permute-done.5.near_ref, bf16[16,8,256]{2,1,0:T(8,128)(2,1)S(1)} %collective-permute-done.6.far_ref, bf16[3,144,256]{2,1,0:T(8,128)(2,1)S(1)} %collective-permute-done.7.south_ref, ...), custom_call_target="tpu_custom_call" | custom-call | flops 7000000000 | bytes 4000000 | tf_op jit(solution)/shard_map/backward/pallas_call | solution.py:538
  107.0 3.3 %all-to-all-done.1 = bf16[64,8,640]{2,1,0:T(8,128)(2,1)S(1)} async-done(((bf16[64,8,640]{2,1,0:T(8,128)(2,1)}), bf16[64,8,640]{2,1,0:T(8,128)(2,1)S(1)}, u32[]{:S(2)}, u32[]{:S(2)}) %all-to-all-start.1) | async-done | bytes 655392 | tf_op jit(solution)/shard_map/all_to_all | solution.py:535
  110.3 2.1 %collective-permute-done.9 = bf16[64,8,640]{2,1,0:T(8,128)(2,1)S(1)} collective-permute-done((bf16[64,8,640]{2,1,0:T(8,128)(2,1)S(1)}, bf16[64,8,640]{2,1,0:T(8,128)(2,1)S(1)}, u32[]{:S(2)}, u32[]{:S(2)}) %collective-permute-start.9) | collective-permute-done | bytes 655392 | tf_op jit(solution)/shard_map/ppermute | solution.py:551
  113.0 0.6 slice_bitcast_fusion
  113.6 0.6 reshape.53
  114.2 1.2 %fusion.1 = (f32[1,32,8,2,512]{4,2,3,1,0:T(8,128)S(1)}, f32[1,32,8,2,512]{4,2,3,1,0:T(8,128)}) fusion(f32[2,32,8,2,512]{4,2,3,1,0:T(8,128)S(1)} %bitcast.21), kind=kLoop, calls=%fused_computation.27 | loop fusion | bytes 4194304 | tf_op jit(solution)/shard_map/slice | solution.py:564
  115.4 1.3 %copy.24 = f32[1024,256]{1,0:T(8,128)} copy(f32[1024,256]{0,1:T(8,128)S(1)} %bitcast.22) | data formatting | bytes 2097152
  (37 shorter events, 0.9 us)
Async XLA Ops:
  0.6 14.4 %copy-start.3 = (bf16[256,1024]{1,0:T(8,128)(2,1)S(1)}, bf16[256,1024]{1,0:T(8,128)(2,1)}, u32[]{:S(2)}) copy-start(bf16[256,1024]{1,0:T(8,128)(2,1)} %w_in_ref.1) | copy-start | bytes 1572868
  0.6 15.4 %copy-start.4 = (bf16[1024,256]{1,0:T(8,128)(2,1)S(1)}, bf16[1024,256]{1,0:T(8,128)(2,1)}, u32[]{:S(2)}) copy-start(bf16[1024,256]{1,0:T(8,128)(2,1)} %w_out_ref.1) | copy-start | bytes 1572868
  1.6 7.6 %collective-permute-start.1 = (bf16[16,8,256]{2,1,0:T(8,128)(2,1)S(1)}, bf16[16,8,256]{2,1,0:T(8,128)(2,1)S(1)}, u32[]{:S(2)}, u32[]{:S(2)}) collective-permute-start(bf16[16,8,256]{2,1,0:T(8,128)(2,1)S(1)} %get-tuple-element.46), channel_id=1, source_target_pairs={{8,16},{24,32},{40,48},{56,64},{72,80},{88,96},{104,112},{120,0},{... | collective-permute-start | bytes 196616 | tf_op jit(solution)/shard_map/ppermute | solution.py:432
  7.3 2.0 %collective-permute-start = (bf16[16,8,256]{2,1,0:T(8,128)(2,1)S(1)}, bf16[16,8,256]{2,1,0:T(8,128)(2,1)S(1)}, u32[]{:S(2)}, u32[]{:S(2)}) collective-permute-start(bf16[16,8,256]{2,1,0:T(8,128)(2,1)S(1)} %get-tuple-element.47), channel_id=1, source_target_pairs={{0,8},{8,0},{1,9},{9,1},{2,10},{10,2},{3,11},{11,3},{4,12},{12,4},... | collective-permute-start | bytes 196616 | tf_op jit(solution)/shard_map/ppermute | solution.py:433
  9.3 9.2 %copy-start.5 = (bf16[16,8,256]{2,1,0:T(8,128)(2,1)}, bf16[16,8,256]{2,1,0:T(8,128)(2,1)S(1)}, u32[]{:S(2)}) copy-start(bf16[16,8,256]{2,1,0:T(8,128)(2,1)S(1)} %collective-permute-done.1.far_ref) | copy-start | bytes 196612
  9.3 9.2 %copy-start.6 = (bf16[16,8,256]{2,1,0:T(8,128)(2,1)}, bf16[16,8,256]{2,1,0:T(8,128)(2,1)S(1)}, u32[]{:S(2)}) copy-start(bf16[16,8,256]{2,1,0:T(8,128)(2,1)S(1)} %collective-permute-done.near_ref) | copy-start | bytes 196612
  9.3 9.2 %collective-permute-start.2 = (bf16[3,144,256]{2,1,0:T(8,128)(2,1)S(1)}, bf16[3,144,256]{2,1,0:T(8,128)(2,1)S(1)}, u32[]{:S(2)}, u32[]{:S(2)}) collective-permute-start(bf16[3,144,256]{2,1,0:T(8,128)(2,1)S(1)} %pad_maximum_fusion.1), channel_id=1, source_target_pairs={{0,1},{1,2},{2,3},{3,4},{4,5},{5,6},{6,7},{7,0},{8,9},{9,10},{10,1... | collective-permute-start | bytes 663560 | tf_op jit(solution)/shard_map/ppermute | solution.py:453
  11.0 7.5 %collective-permute-start.3 = (bf16[3,144,256]{2,1,0:T(8,128)(2,1)S(1)}, bf16[3,144,256]{2,1,0:T(8,128)(2,1)S(1)}, u32[]{:S(2)}, u32[]{:S(2)}) collective-permute-start(bf16[3,144,256]{2,1,0:T(8,128)(2,1)S(1)} %pad_maximum_fusion.2), channel_id=1, source_target_pairs={{0,7},{1,0},{2,1},{3,2},{4,3},{5,4},{6,5},{7,6},{8,15},{9,8},{10,9... | collective-permute-start | bytes 663560 | tf_op jit(solution)/shard_map/ppermute | solution.py:453
  18.5 0.7 copy-start.7
  18.5 0.8 copy-start.8
  55.0 6.6 %collective-permute-start.4 = (bf16[64,8,640]{2,1,0:T(8,128)(2,1)}, bf16[64,8,640]{2,1,0:T(8,128)(2,1)S(1)}, u32[]{:S(2)}, u32[]{:S(2)}) collective-permute-start(bf16[64,8,640]{2,1,0:T(8,128)(2,1)} %get-tuple-element.20), channel_id=1, source_target_pairs={{0,8},{8,0},{1,9},{9,1},{2,10},{10,2},{3,11},{11,3},{4,12},{12,4},... | collective-permute-start | bytes 1966088 | tf_op jit(solution)/shard_map/ppermute | solution.py:522
  55.9 14.9 %collective-permute-start.6 = (bf16[16,8,256]{2,1,0:T(8,128)(2,1)S(1)}, bf16[16,8,256]{2,1,0:T(8,128)(2,1)S(1)}, u32[]{:S(2)}, u32[]{:S(2)}) collective-permute-start(bf16[16,8,256]{2,1,0:T(8,128)(2,1)S(1)} %get-tuple-element.42), channel_id=1, source_target_pairs={{8,16},{24,32},{40,48},{56,64},{72,80},{88,96},{104,112},{120,0},{... | collective-permute-start | bytes 196616 | tf_op jit(solution)/shard_map/ppermute | solution.py:432
  60.6 10.3 %collective-permute-start.5 = (bf16[16,8,256]{2,1,0:T(8,128)(2,1)S(1)}, bf16[16,8,256]{2,1,0:T(8,128)(2,1)S(1)}, u32[]{:S(2)}, u32[]{:S(2)}) collective-permute-start(bf16[16,8,256]{2,1,0:T(8,128)(2,1)S(1)} %get-tuple-element.43), channel_id=1, source_target_pairs={{0,8},{8,0},{1,9},{9,1},{2,10},{10,2},{3,11},{11,3},{4,12},{12,4},... | collective-permute-start | bytes 196616 | tf_op jit(solution)/shard_map/ppermute | solution.py:433
  63.7 22.3 %all-to-all-start = ((bf16[64,8,640]{2,1,0:T(8,128)(2,1)}), bf16[64,8,640]{2,1,0:T(8,128)(2,1)S(1)}, u32[]{:S(2)}, u32[]{:S(2)}) async-start(bf16[64,8,640]{2,1,0:T(8,128)(2,1)} %add_convert_fusion), calls=%async_computation | async-start | bytes 1310720 | tf_op jit(solution)/shard_map/all_to_all | solution.py:524
  70.8 24.9 %copy-start = (bf16[16,128,256]{2,1,0:T(8,128)(2,1)S(1)}, bf16[16,128,256]{2,1,0:T(8,128)(2,1)}, u32[]{:S(2)}) copy-start(bf16[16,128,256]{2,1,0:T(8,128)(2,1)} %get-tuple-element.23.main_ref) | copy-start | bytes 3145732
  70.8 24.9 %copy-start.1 = (bf16[16,128,256]{2,1,0:T(8,128)(2,1)S(1)}, bf16[16,128,256]{2,1,0:T(8,128)(2,1)}, u32[]{:S(2)}) copy-start(bf16[16,128,256]{2,1,0:T(8,128)(2,1)} %cot_ref.3) | copy-start | bytes 3145732
  70.8 24.9 %copy-start.2 = (f32[7,7,256]{2,1,0:T(8,128)S(1)}, f32[7,7,256]{2,1,0:T(8,128)}, u32[]{:S(2)}) copy-start(f32[7,7,256]{2,1,0:T(8,128)} %taps_ref.3) | copy-start | bytes 150532
  71.6 15.6 %collective-permute-start.7 = (bf16[3,144,256]{2,1,0:T(8,128)(2,1)}, bf16[3,144,256]{2,1,0:T(8,128)(2,1)S(1)}, u32[]{:S(2)}, u32[]{:S(2)}) collective-permute-start(bf16[3,144,256]{2,1,0:T(8,128)(2,1)} %pad_maximum_fusion.3), channel_id=1, source_target_pairs={{0,1},{1,2},{2,3},{3,4},{4,5},{5,6},{6,7},{7,0},{8,9},{9,10},{10,1... | collective-permute-start | bytes 663560 | tf_op jit(solution)/shard_map/ppermute | solution.py:453
  73.8 13.3 %collective-permute-start.8 = (bf16[3,144,256]{2,1,0:T(8,128)(2,1)}, bf16[3,144,256]{2,1,0:T(8,128)(2,1)S(1)}, u32[]{:S(2)}, u32[]{:S(2)}) collective-permute-start(bf16[3,144,256]{2,1,0:T(8,128)(2,1)} %pad_maximum_fusion.4), channel_id=1, source_target_pairs={{0,7},{1,0},{2,1},{3,2},{4,3},{5,4},{6,5},{7,6},{8,15},{9,8},{10,9... | collective-permute-start | bytes 663560 | tf_op jit(solution)/shard_map/ppermute | solution.py:453
  88.1 22.3 %all-to-all-start.1 = ((bf16[64,8,640]{2,1,0:T(8,128)(2,1)}), bf16[64,8,640]{2,1,0:T(8,128)(2,1)S(1)}, u32[]{:S(2)}, u32[]{:S(2)}) async-start(bf16[64,8,640]{2,1,0:T(8,128)(2,1)} %broadcast_in_dim.2), calls=%async_computation.1 | async-start | bytes 1310720 | tf_op jit(solution)/shard_map/all_to_all | solution.py:535
  110.3 2.1 %collective-permute-start.9 = (bf16[64,8,640]{2,1,0:T(8,128)(2,1)S(1)}, bf16[64,8,640]{2,1,0:T(8,128)(2,1)S(1)}, u32[]{:S(2)}, u32[]{:S(2)}) collective-permute-start(bf16[64,8,640]{2,1,0:T(8,128)(2,1)S(1)} %all-to-all-done.1), channel_id=1, source_target_pairs={{0,8},{8,0},{1,9},{9,1},{2,10},{10,2},{3,11},{11,3},{4,12},{12,4},... | collective-permute-start | bytes 1966088 | tf_op jit(solution)/shard_map/ppermute | solution.py:551

commit v3 on v2

--- a/solution.py
+++ b/solution.py
@@ -16,7 +16,7 @@
 SPAN = 16
 EDGE = 8
 SLOTS = 64
-FORWARD_VMEM = 56 * 1024 * 1024
+FORWARD_VMEM = 36 * 1024 * 1024
 BACKWARD_VMEM = 28 * 1024 * 1024
 GROUP = 4
 CUTS = ((0, 2), (2, 4), (4, 7))
@@ -34,6 +34,10 @@
 
 def dot(a, b):
     return jnp.dot(a, b, preferred_element_type=F32)
+
+
+def dot_flipped(a, b):
+    return lax.dot_general(a, b, (((1,), (1,)), ((), ())), preferred_element_type=F32)
 
 
 def build_weights(taps_ref, w_ref, flip):
@@ -61,7 +65,7 @@
                         ] = block.astype(BF16)
 
 
-def assemble(main_ref, near_ref, far_ref, south_ref, north_ref, wide, xs):
+def assemble(main_ref, near_ref, far_ref, south_ref, north_ref, wide, xs, xs_wide=None):
     rows, tile, _ = main_ref.shape
     even = lax.axis_index("core") == 0
     band = lax.axis_index(LAT)
@@ -90,6 +94,8 @@
             for h in range(2):
                 for t in range(STEP + 2 * MARGIN):
                     piece = wide[h, r, pl.ds(EDGE - MARGIN + t, SPAN, stride=STEP), :]
+                    if xs_wide is not None:
+                        xs_wide[h, r, t] = piece
                     xs[h, r, t] = piece.astype(BF16)
         return 0
 
@@ -138,28 +144,23 @@
     return dot(jnp.concatenate(pieces, axis=1), w_ref[h])
 
 
-def tap_part(gm_xs, wide, h, i, b, side, pair, sums):
+def tap_part(gm_xs, xs_wide, h, i, b, side, pair, sums):
     source = jnp.maximum(pair, 0)
     part = slice(side * 8, side * 8 + 8)
     grads = [gm_xs[h, 2 * pair + 2 + b, t, part] for t in range(STEP)]
     for spot in range(STEP + KS - 1):
-        cell = wide[
-            h,
-            2 * source + b + i,
-            pl.ds(EDGE - MARGIN + spot + side * 8 * STEP, 8, stride=STEP),
-            :,
-        ]
+        cell = xs_wide[h, 2 * source + b + i, spot, part]
         for j in range(KS):
             if 0 <= spot - j < STEP:
                 sums[j] = sums[j] + grads[spot - j] * cell
     return sums
 
 
-def add_taps(gm_xs, wide, acc_taps, h, i, pair):
+def add_taps(gm_xs, xs_wide, acc_taps, h, i, pair):
     sums = [acc_taps[h, i * KS + j] for j in range(KS)]
     for b in range(2):
         for side in range(2):
-            sums = tap_part(gm_xs, wide, h, i, b, side, pair, sums)
+            sums = tap_part(gm_xs, xs_wide, h, i, b, side, pair, sums)
     for j in range(KS):
         acc_taps[h, i * KS + j] = sums[j]
 
@@ -215,10 +216,8 @@
     gain_ref,
     bias_ref,
     w_in_ref,
-    w_in_t_ref,
     b_in_ref,
     w_out_ref,
-    w_out_t_ref,
     scale_ref,
     out_ref,
     gm_ref,
@@ -226,6 +225,7 @@
     send_ref,
     wide,
     xs,
+    xs_wide,
     w_ref,
     out_wide,
     gm_wide,
@@ -242,7 +242,7 @@
     width = 2 * HALF
     cells = 2 * STEP * SPAN
     build_weights(taps_ref, w_ref, False)
-    assemble(main_ref, near_ref, far_ref, south_ref, north_ref, wide, xs)
+    assemble(main_ref, near_ref, far_ref, south_ref, north_ref, wide, xs, xs_wide)
     stage_cotangent(cot_ref, sea_ref, slot_ref, SLOTS, out_wide, mask_wide)
     acc_in[...] = jnp.zeros_like(acc_in)
     acc_out[...] = jnp.zeros_like(acc_out)
@@ -272,7 +272,7 @@
             axis=0,
         )
         later = jnp.minimum(pair + 1, rows // 2 - 1)
-        conv_tasks, tap_tasks = [], []
+        conv_tasks, sum_tasks = [], []
         for h in range(2):
             begun = {}
 
@@ -286,10 +286,10 @@
                 for first, last in CUTS:
                     conv_tasks.append(functools.partial(conv_task, h, i2, first, last, begun))
             for i in range(KS):
-                tap_tasks.append(
-                    functools.partial(add_taps, gm_xs, wide, acc_taps, h, i, pair - 1)
+                sum_tasks.append(
+                    functools.partial(add_taps, gm_xs, xs_wide, acc_taps, h, i, pair - 1)
                 )
-        for work in zipped(conv_tasks, tap_tasks):
+        for work in zipped(conv_tasks, sum_tasks):
             work()
         mean = jnp.mean(mixed, axis=1, keepdims=True)
         centered = mixed - mean
@@ -314,7 +314,7 @@
             part = slice(f * 256, (f + 1) * 256)
             return (
                 dot(normalized, w_in_ref[:, part]) + b_in_ref[:, part],
-                dot(grad_out, w_out_t_ref[:, part]),
+                dot_flipped(grad_out, w_out_ref[part, :]),
             )
 
         ahead = enter(0)
@@ -333,7 +333,7 @@
             act_low = act.astype(BF16)
             grad_hidden = (grad_act * slope).astype(BF16)
             branch = branch + dot(act_low, w_out_ref[part, :])
-            grad_norm = grad_norm + dot(grad_hidden, w_in_t_ref[part, :])
+            grad_norm = grad_norm + dot_flipped(grad_hidden, w_in_ref[:, part])
             acc_in[:, part] += dot(normalized_t, grad_hidden)
             acc_out[:, part] += dot(grad_out_t, act_low)
         branch = branch.astype(BF16).astype(F32)
@@ -353,7 +353,7 @@
                 row = 2 * pair + b
                 for t in range(STEP):
                     start = b * STEP * SPAN + t * SPAN
-                    feature = wide[h, row + MARGIN, pl.ds(EDGE + t, SPAN, stride=STEP), :]
+                    feature = xs_wide[h, row + MARGIN, t + MARGIN]
                     out_wide[h, row, pl.ds(t, SPAN, stride=STEP), :] = (
                         feature + added[start : start + SPAN]
                     )
@@ -367,7 +367,7 @@
     finish(rows // 2 - 1)
     for h in range(2):
         for i in range(KS):
-            add_taps(gm_xs, wide, acc_taps, h, i, rows // 2 - 1)
+            add_taps(gm_xs, xs_wide, acc_taps, h, i, rows // 2 - 1)
     core = lax.axis_index("core")
 
     @pl.when(core == 0)
@@ -477,11 +477,12 @@
             jax.ShapeDtypeStruct((chips, 8, chunk), BF16),
             jax.ShapeDtypeStruct((chips, 8, chunk), BF16),
         ),
-        in_specs=[vmem] * 17,
+        in_specs=[vmem] * 15,
         out_specs=(vmem,) * 4,
         scratch_shapes=[
             wide,
             xs,
+            pltpu.VMEM((2, padded, ext, SPAN, HALF), F32),
             weights,
             flat,
             flat,
@@ -511,15 +512,14 @@
         ln_gain.reshape(1, width),
         ln_bias.reshape(1, width),
         w_in,
-        w_in.T,
         b_in.reshape(1, ff),
         w_out,
-        w_out.T,
         layer_scale.reshape(1, width),
     )
     swap = [(0, 1), (1, 0)]
+    sums = (keep.astype(F32) + lax.ppermute(send, "core", swap).astype(F32)).astype(BF16)
+    sums, grad_mixed = lax.optimization_barrier((sums, grad_mixed))
     near, far = rim_sides(grad_mixed)
-    sums = (keep.astype(F32) + lax.ppermute(send, "core", swap).astype(F32)).astype(BF16)
     south, north = rim_ends(*rim_messages(grad_mixed, near, far))
     arrived = lax.all_to_all(sums, CHIPS, split_axis=0, concat_axis=0, tiled=True)
     own, grad_mixed, near, far, south, north = lax.optimization_barrier(
@@ -549,22 +549,75 @@
     )(grad_mixed, near, far, south, north, cotangent, kernel)
     mine, grad_features = lax.optimization_barrier((mine, grad_features))
     other = lax.ppermute(mine, "core", swap)
-    first = lax.axis_index("core") == 0
-    whole = jnp.stack([jnp.where(first, mine, other), jnp.where(first, other, mine)])
     factor = 1.0 / math.sqrt(rows * lax.axis_size(LAT) * tile * lax.axis_size(LON))
-    main = whole[..., : ff // 2].reshape(2, width // 8, 2, 8, ff // 2)
-    main = main.transpose(0, 1, 3, 2, 4).reshape(2, width, ff).astype(F32) * factor
-    small = whole[..., ff // 2 :].reshape(2 * chips, 8, HALF)[: 2 * (KS * KS + 1)]
-    small = jnp.sum(small.astype(F32), axis=1) * factor
-    small = small.reshape(KS * KS + 1, width)
+    grad_in, grad_out, grad_taps, grad_scale = pl.pallas_call(
+        functools.partial(unpack_kernel, factor),
+        out_shape=(
+            jax.ShapeDtypeStruct((width, ff), F32),
+            jax.ShapeDtypeStruct((ff, width), F32),
+            jax.ShapeDtypeStruct(kernel.shape, F32),
+            jax.ShapeDtypeStruct((1, width), F32),
+        ),
+        in_specs=[vmem] * 2,
+        out_specs=(vmem,) * 4,
+        compiler_params=pltpu.CompilerParams(vmem_limit_bytes=BACKWARD_VMEM),
+        name="unpack",
+    )(mine, other)
     return (
         output,
         grad_features,
-        main[0],
-        main[1].T,
-        small[: KS * KS].reshape(KS, KS, width),
-        small[KS * KS],
+        grad_in,
+        grad_out,
+        grad_taps,
+        grad_scale.reshape(width),
     )
+
+
+def unpack_kernel(factor, mine_ref, other_ref, grad_in_ref, grad_out_ref, taps_ref, scale_ref):
+    half_ff = grad_in_ref.shape[1] // 2
+    spots = mine_ref.shape[0]
+
+    def unpack(first_ref, second_ref):
+        def quad(n, _):
+            for g in range(2):
+                for side in range(2):
+                    group = 2 * n + g
+                    columns = slice(side * half_ff, (side + 1) * half_ff)
+                    grad_in_ref[pl.ds(pl.multiple_of(group * 8, 8), 8), columns] = (
+                        first_ref[group * 2 + side, :, :half_ff].astype(F32) * factor
+                    )
+            return 0
+
+        lax.fori_loop(0, spots // 4, quad, 0)
+        for block in range(grad_out_ref.shape[1] // HALF):
+            for side in range(2):
+                rows = [
+                    second_ref[(block * SPAN + n) * 2 + side, :, :half_ff].astype(F32)
+                    for n in range(SPAN)
+                ]
+                grad_out_ref[
+                    side * half_ff : (side + 1) * half_ff, block * HALF : (block + 1) * HALF
+                ] = jnp.concatenate(rows, axis=0).T * factor
+        for spot in range(2 * (KS * KS + 1)):
+            ref = first_ref if spot < spots else second_ref
+            tap, h = spot // 2, spot % 2
+            part = ref[spot % spots, :, half_ff:].astype(F32)
+            lanes = slice(h * HALF, (h + 1) * HALF)
+            total = jnp.sum(part, axis=0, keepdims=True) * factor
+            if tap < KS * KS:
+                taps_ref[tap // KS, tap % KS : tap % KS + 1, lanes] = total
+            else:
+                scale_ref[:, lanes] = total
+
+    core = lax.axis_index("core")
+
+    @pl.when(core == 0)
+    def _():
+        unpack(mine_ref, other_ref)
+
+    @pl.when(core != 0)
+    def _():
+        unpack(other_ref, mine_ref)
 
 
 def solution(mesh):

time: 118 us -> 113 us (0.958)
  local copies, waits for them, and re-layouts: 10.8 us -> 4.35 us
  waiting for transfers between devices: 18.3 us -> 23.4 us
  other arithmetic: 6.07 us -> 3.57 us
  Pallas kernels: 47.1 us -> 45.5 us
    ppermute x4, waiting for transfers between devices: 2.5 us -> 5.83 us  [rim_ends(): return (lax.ppermute(up, LAT, forward), lax.ppermute(down, LAT, backward))]
    pallas_call x1, Pallas kernels: 35.8 us -> 32.5 us  [on_device(): pl.pallas_call(forward_kernel, out_shape=(jax.ShapeDtypeStruct(features.s...]
    unnamed x22 -> x25, local copies, waits for them, and re-layouts: 5.44 us -> 2.39 us
    ppermute x1, waiting for transfers between devices: 0.01 us -> 2.09 us  [on_device(): lax.ppermute(send, 'core', swap).astype(F32)]
    pallas_call x0 -> x1, Pallas kernels: none -> 1.77 us  [on_device(): pl.pallas_call(functools.partial(unpack_kernel, factor), out_shape=(jax.S...]
    slice x1 -> x0, local copies, waits for them, and re-layouts: 1.22 us -> none  [on_device(): main[1]]
  transfers between devices with their start and end apart: 12 -> 12, of which waited for: 6 -> 7; matrix products, arithmetic and copies ran while one was open for 9% -> 2% of each run, Pallas kernels for 10% -> 10%
where the time goes in v3:
time: 113 us; the launch traced here: 111 us
  Pallas kernels  45.5 us (40%)
  starting transfers between devices  33.4 us (30%)
  waiting for transfers between devices  23.4 us (21%)
  local copies, waits for them, and re-layouts  4.35 us (4%)
  other arithmetic  3.57 us (3%)
    pallas_call x1, Pallas kernels, on_device(): pl.pallas_call(forward_kernel, out_shape=(jax.ShapeDtypeStruct(features.s...  32.5 us
    pallas_call x1, Pallas kernels, on_device(): pl.pallas_call(backward_kernel, out_shape=jax.ShapeDtypeStruct(features.s...  11.3 us
    ppermute x2, starting transfers between devices, rim_sides(): far = lax.ppermute(jnp.where(even, low, high), LON, across)  10.3 us
    all_to_all x1, waiting for transfers between devices, on_device(): lax.all_to_all(sums, CHIPS, split_axis=0, concat_axis=0, tiled=True)  9.3 us
    ppermute x4, starting transfers between devices, rim_ends(): return (lax.ppermute(up, LAT, forward), lax.ppermute(down, LAT, backward))  8.5 us
    all_to_all x1, starting transfers between devices, on_device(): lax.all_to_all(jnp.broadcast_to(own[None], (chips,) + own.shape), CHIPS,...  7.48 us
    all_to_all x1, starting transfers between devices, on_device(): lax.all_to_all(sums, CHIPS, split_axis=0, concat_axis=0, tiled=True)  7.11 us
    ppermute x4, waiting for transfers between devices, rim_ends(): return (lax.ppermute(up, LAT, forward), lax.ppermute(down, LAT, backward))  5.83 us
  transfers between devices with their start and end apart: 12, of which 7 were waited for; matrix products, arithmetic and copies ran while one was open for 2% of the time, Pallas kernels for 10%

profile of v3, /device:TPU:0, one launch (start us, length us, event | category | flops | bytes accessed | tf_op | source)
XLA Modules:
  0.0 111.2 jit_solution(9619814974883356365)
XLA Ops:
  0.6 0.0 copy-start
  0.7 1.0 broadcast_select_fusion.2
  1.7 5.7 %collective-permute-start.1 = (bf16[16,8,256]{2,1,0:T(8,128)(2,1)S(1)}, bf16[16,8,256]{2,1,0:T(8,128)(2,1)S(1)}, u32[]{:S(2)}, u32[]{:S(2)}) collective-permute-start(bf16[16,8,256]{2,1,0:T(8,128)(2,1)S(1)} %get-tuple-element.48), channel_id=1, source_target_pairs={{8,16},{24,32},{40,48},{56,64},{72,80},{88,96},{104,112},{120,0},{... | collective-permute-start | bytes 196616 | tf_op jit(solution)/shard_map/ppermute | solution.py:432
  7.4 0.0 collective-permute-start
  7.4 1.0 fusion.1
  8.5 0.9 collective-permute-done.1.far_ref
  9.3 0.0 collective-permute-done.near_ref
  9.4 1.6 %collective-permute-start.2 = (bf16[3,144,256]{2,1,0:T(8,128)(2,1)S(1)}, bf16[3,144,256]{2,1,0:T(8,128)(2,1)S(1)}, u32[]{:S(2)}, u32[]{:S(2)}) collective-permute-start(bf16[3,144,256]{2,1,0:T(8,128)(2,1)S(1)} %pad_maximum_fusion), channel_id=1, source_target_pairs={{0,1},{1,2},{2,3},{3,4},{4,5},{5,6},{6,7},{7,0},{8,9},{9,10},{10,1... | collective-permute-start | bytes 663560 | tf_op jit(solution)/shard_map/ppermute | solution.py:453
  11.1 2.7 %collective-permute-start.3 = (bf16[3,144,256]{2,1,0:T(8,128)(2,1)S(1)}, bf16[3,144,256]{2,1,0:T(8,128)(2,1)S(1)}, u32[]{:S(2)}, u32[]{:S(2)}) collective-permute-start(bf16[3,144,256]{2,1,0:T(8,128)(2,1)S(1)} %pad_maximum_fusion.1), channel_id=1, source_target_pairs={{0,7},{1,0},{2,1},{3,2},{4,3},{5,4},{6,5},{7,6},{8,15},{9,8},{10,9... | collective-permute-start | bytes 663560 | tf_op jit(solution)/shard_map/ppermute | solution.py:453
  13.8 0.1 copy.17.slot_ref
  13.9 4.7 %collective-permute-done.2.south_ref = bf16[3,144,256]{2,1,0:T(8,128)(2,1)S(1)} collective-permute-done((bf16[3,144,256]{2,1,0:T(8,128)(2,1)S(1)}, bf16[3,144,256]{2,1,0:T(8,128)(2,1)S(1)}, u32[]{:S(2)}, u32[]{:S(2)}) %collective-permute-start.2) | collective-permute-done | bytes 221216 | tf_op jit(solution)/shard_map/ppermute | solution.py:453
  18.6 0.0 copy-start.1
  18.6 1.2 %copy-done.1 = bf16[16,128,256]{2,1,0:T(8,128)(2,1)S(1)} copy-done((bf16[16,128,256]{2,1,0:T(8,128)(2,1)S(1)}, bf16[16,128,256]{2,1,0:T(8,128)(2,1)}, u32[]{:S(2)}) %copy-start.1) | copy-done | bytes 1048600
  19.8 1.0 copy-done.4
  20.9 32.5 %forward.1 = (bf16[16,128,256]{2,1,0:T(8,128)(2,1)}, bf16[16,128,256]{2,1,0:T(8,128)(2,1)S(1)}, bf16[64,8,640]{2,1,0:T(8,128)(2,1)S(1)}, bf16[64,8,640]{2,1,0:T(8,128)(2,1)S(1)}) custom-call(bf16[16,128,256]{2,1,0:T(8,128)(2,1)S(1)} %copy-done, bf16[16,8,256]{2,1,0:T(8,128)(2,1)S(1)} %collective-permute-done.near_ref, ...), custom_call_target="tpu_custom_call" | custom-call | flops 14000000000 | bytes 8000000 | tf_op jit(solution)/shard_map/forward/pallas_call | solution.py:472
  53.4 2.1 %collective-permute-done.4 = bf16[64,8,640]{2,1,0:T(8,128)(2,1)S(1)} collective-permute-done((bf16[64,8,640]{2,1,0:T(8,128)(2,1)S(1)}, bf16[64,8,640]{2,1,0:T(8,128)(2,1)S(1)}, u32[]{:S(2)}, u32[]{:S(2)}) %collective-permute-start.4) | collective-permute-done | bytes 655392 | tf_op jit(solution)/shard_map/ppermute | solution.py:520
  55.5 1.0 add_convert_fusion
  56.5 4.6 %collective-permute-start.6 = (bf16[16,8,256]{2,1,0:T(8,128)(2,1)S(1)}, bf16[16,8,256]{2,1,0:T(8,128)(2,1)S(1)}, u32[]{:S(2)}, u32[]{:S(2)}) collective-permute-start(bf16[16,8,256]{2,1,0:T(8,128)(2,1)S(1)} %get-tuple-element.44), channel_id=1, source_target_pairs={{8,16},{24,32},{40,48},{56,64},{72,80},{88,96},{104,112},{120,0},{... | collective-permute-start | bytes 196616 | tf_op jit(solution)/shard_map/ppermute | solution.py:432
  61.2 7.1 %all-to-all-start = ((bf16[64,8,640]{2,1,0:T(8,128)(2,1)}), bf16[64,8,640]{2,1,0:T(8,128)(2,1)S(1)}, u32[]{:S(2)}, u32[]{:S(2)}) async-start(bf16[64,8,640]{2,1,0:T(8,128)(2,1)} %add_convert_fusion), calls=%async_computation | async-start | bytes 1310720 | tf_op jit(solution)/shard_map/all_to_all | solution.py:524
  68.3 0.7 pad_maximum_fusion.2
  69.0 1.6 %collective-permute-start.7 = (bf16[3,144,256]{2,1,0:T(8,128)(2,1)}, bf16[3,144,256]{2,1,0:T(8,128)(2,1)S(1)}, u32[]{:S(2)}, u32[]{:S(2)}) collective-permute-start(bf16[3,144,256]{2,1,0:T(8,128)(2,1)} %pad_maximum_fusion.2), channel_id=1, source_target_pairs={{0,1},{1,2},{2,3},{3,4},{4,5},{5,6},{6,7},{7,0},{8,9},{9,10},{10,1... | collective-permute-start | bytes 663560 | tf_op jit(solution)/shard_map/ppermute | solution.py:453
  70.6 0.7 pad_maximum_fusion.3
  71.3 2.6 %collective-permute-start.8 = (bf16[3,144,256]{2,1,0:T(8,128)(2,1)}, bf16[3,144,256]{2,1,0:T(8,128)(2,1)S(1)}, u32[]{:S(2)}, u32[]{:S(2)}) collective-permute-start(bf16[3,144,256]{2,1,0:T(8,128)(2,1)} %pad_maximum_fusion.3), channel_id=1, source_target_pairs={{0,7},{1,0},{2,1},{3,2},{4,3},{5,4},{6,5},{7,6},{8,15},{9,8},{10,9... | collective-permute-start | bytes 663560 | tf_op jit(solution)/shard_map/ppermute | solution.py:453
  73.8 9.3 %all-to-all-done = bf16[64,8,640]{2,1,0:T(8,128)(2,1)S(1)} async-done(((bf16[64,8,640]{2,1,0:T(8,128)(2,1)}), bf16[64,8,640]{2,1,0:T(8,128)(2,1)S(1)}, u32[]{:S(2)}, u32[]{:S(2)}) %all-to-all-start) | async-done | bytes 655392 | tf_op jit(solution)/shard_map/all_to_all | solution.py:524
  83.1 0.1 reduce_sum.12
  83.3 1.2 %collective-permute-done.7.south_ref = bf16[3,144,256]{2,1,0:T(8,128)(2,1)S(1)} collective-permute-done((bf16[3,144,256]{2,1,0:T(8,128)(2,1)}, bf16[3,144,256]{2,1,0:T(8,128)(2,1)S(1)}, u32[]{:S(2)}, u32[]{:S(2)}) %collective-permute-start.7) | collective-permute-done | bytes 221216 | tf_op jit(solution)/shard_map/ppermute | solution.py:453
  84.4 0.9 broadcast_in_dim.2
  85.3 7.5 %all-to-all-start.1 = ((bf16[64,8,640]{2,1,0:T(8,128)(2,1)}), bf16[64,8,640]{2,1,0:T(8,128)(2,1)S(1)}, u32[]{:S(2)}, u32[]{:S(2)}) async-start(bf16[64,8,640]{2,1,0:T(8,128)(2,1)} %broadcast_in_dim.2), calls=%async_computation.1 | async-start | bytes 1310720 | tf_op jit(solution)/shard_map/all_to_all | solution.py:535
  92.8 11.3 %backward.1 = bf16[16,128,256]{2,1,0:T(8,128)(2,1)} custom-call(bf16[16,128,256]{2,1,0:T(8,128)(2,1)S(1)} %get-tuple-element.31.main_ref, bf16[16,8,256]{2,1,0:T(8,128)(2,1)S(1)} %collective-permute-done.5.near_ref, bf16[16,8,256]{2,1,0:T(8,128)(2,1)S(1)} %collective-permute-done.6.far_ref, bf16[3,144,256]{2,1,0:T(8,128)(2,1)S(1)} %collective-permute-done.7.south_ref, ...), custom_call_target="tpu_custom_call" | custom-call | flops 7000000000 | bytes 4000000 | tf_op jit(solution)/shard_map/backward/pallas_call | solution.py:538
  104.1 3.2 %all-to-all-done.1.mine_ref = bf16[64,8,640]{2,1,0:T(8,128)(2,1)S(1)} async-done(((bf16[64,8,640]{2,1,0:T(8,128)(2,1)}), bf16[64,8,640]{2,1,0:T(8,128)(2,1)S(1)}, u32[]{:S(2)}, u32[]{:S(2)}) %all-to-all-start.1) | async-done | bytes 655392 | tf_op jit(solution)/shard_map/all_to_all | solution.py:535
  107.3 2.1 %collective-permute-done.9.other_ref = bf16[64,8,640]{2,1,0:T(8,128)(2,1)S(1)} collective-permute-done((bf16[64,8,640]{2,1,0:T(8,128)(2,1)S(1)}, bf16[64,8,640]{2,1,0:T(8,128)(2,1)S(1)}, u32[]{:S(2)}, u32[]{:S(2)}) %collective-permute-start.9) | collective-permute-done | bytes 655392 | tf_op jit(solution)/shard_map/ppermute | solution.py:551
  109.4 1.8 %unpack.1 = (f32[256,1024]{1,0:T(8,128)}, f32[1024,256]{1,0:T(8,128)}, f32[7,7,256]{2,1,0:T(8,128)}, f32[1,256]{1,0:T(1,128)}) custom-call(bf16[64,8,640]{2,1,0:T(8,128)(2,1)S(1)} %all-to-all-done.1.mine_ref, bf16[64,8,640]{2,1,0:T(8,128)(2,1)S(1)} %collective-permute-done.9.other_ref), custom_call_target="tpu_custom_call" | custom-call | tf_op jit(solution)/shard_map/unpack/pallas_call | solution.py:553
  (33 shorter events, 0.2 us)
Async XLA Ops:
  0.6 17.9 %copy-start = (bf16[16,128,256]{2,1,0:T(8,128)(2,1)S(1)}, bf16[16,128,256]{2,1,0:T(8,128)(2,1)}, u32[]{:S(2)}) copy-start(bf16[16,128,256]{2,1,0:T(8,128)(2,1)} %main_ref.1) | copy-start | bytes 3145732
  0.6 13.1 %copy-start.11 = (s32[16,1]{0,1:T(1,128)S(1)}, s32[16,1]{0,1:T(1,128)}, u32[]{:S(2)}) copy-start(s32[16,1]{0,1:T(1,128)} %param.14) | copy-start | bytes 196
  0.7 17.9 %copy-start.5 = (f32[7,7,256]{2,1,0:T(8,128)S(1)}, f32[7,7,256]{2,1,0:T(8,128)}, u32[]{:S(2)}) copy-start(f32[7,7,256]{2,1,0:T(8,128)} %taps_ref.3) | copy-start | bytes 150532
  0.7 17.9 %copy-start.10 = (f32[256]{0:T(256)S(1)}, f32[256]{0:T(256)}, u32[]{:S(2)}) copy-start(f32[256]{0:T(256)} %param.21) | copy-start | bytes 3076
  0.7 17.9 %copy-start.7 = (f32[1024]{0:T(1024)S(1)}, f32[1024]{0:T(1024)}, u32[]{:S(2)}) copy-start(f32[1024]{0:T(1024)} %param.19) | copy-start | bytes 12292
  0.7 17.9 %copy-start.3 = (bf16[256,1024]{1,0:T(8,128)(2,1)S(1)}, bf16[256,1024]{1,0:T(8,128)(2,1)}, u32[]{:S(2)}) copy-start(bf16[256,1024]{1,0:T(8,128)(2,1)} %w_in_ref.1) | copy-start | bytes 1572868
  0.7 17.9 %copy-start.9 = (f32[256]{0:T(256)S(1)}, f32[256]{0:T(256)}, u32[]{:S(2)}) copy-start(f32[256]{0:T(256)} %param.17) | copy-start | bytes 3076
  0.7 17.9 %copy-start.8 = (f32[256]{0:T(256)S(1)}, f32[256]{0:T(256)}, u32[]{:S(2)}) copy-start(f32[256]{0:T(256)} %param.16) | copy-start | bytes 3076
  0.7 17.9 %copy-start.6 = (s32[16,128]{1,0:T(8,128)S(1)}, s32[16,128]{1,0:T(8,128)}, u32[]{:S(2)}) copy-start(s32[16,128]{1,0:T(8,128)} %sea_ref.1) | copy-start | bytes 24580
  1.7 7.6 %collective-permute-start.1 = (bf16[16,8,256]{2,1,0:T(8,128)(2,1)S(1)}, bf16[16,8,256]{2,1,0:T(8,128)(2,1)S(1)}, u32[]{:S(2)}, u32[]{:S(2)}) collective-permute-start(bf16[16,8,256]{2,1,0:T(8,128)(2,1)S(1)} %get-tuple-element.48), channel_id=1, source_target_pairs={{8,16},{24,32},{40,48},{56,64},{72,80},{88,96},{104,112},{120,0},{... | collective-permute-start | bytes 196616 | tf_op jit(solution)/shard_map/ppermute | solution.py:432
  7.4 2.0 %collective-permute-start = (bf16[16,8,256]{2,1,0:T(8,128)(2,1)S(1)}, bf16[16,8,256]{2,1,0:T(8,128)(2,1)S(1)}, u32[]{:S(2)}, u32[]{:S(2)}) collective-permute-start(bf16[16,8,256]{2,1,0:T(8,128)(2,1)S(1)} %get-tuple-element.49), channel_id=1, source_target_pairs={{0,8},{8,0},{1,9},{9,1},{2,10},{10,2},{3,11},{11,3},{4,12},{12,4},... | collective-permute-start | bytes 196616 | tf_op jit(solution)/shard_map/ppermute | solution.py:433
  9.4 9.1 %collective-permute-start.2 = (bf16[3,144,256]{2,1,0:T(8,128)(2,1)S(1)}, bf16[3,144,256]{2,1,0:T(8,128)(2,1)S(1)}, u32[]{:S(2)}, u32[]{:S(2)}) collective-permute-start(bf16[3,144,256]{2,1,0:T(8,128)(2,1)S(1)} %pad_maximum_fusion), channel_id=1, source_target_pairs={{0,1},{1,2},{2,3},{3,4},{4,5},{5,6},{6,7},{7,0},{8,9},{9,10},{10,1... | collective-permute-start | bytes 663560 | tf_op jit(solution)/shard_map/ppermute | solution.py:453
  11.1 7.5 %collective-permute-start.3 = (bf16[3,144,256]{2,1,0:T(8,128)(2,1)S(1)}, bf16[3,144,256]{2,1,0:T(8,128)(2,1)S(1)}, u32[]{:S(2)}, u32[]{:S(2)}) collective-permute-start(bf16[3,144,256]{2,1,0:T(8,128)(2,1)S(1)} %pad_maximum_fusion.1), channel_id=1, source_target_pairs={{0,7},{1,0},{2,1},{3,2},{4,3},{5,4},{6,5},{7,6},{8,15},{9,8},{10,9... | collective-permute-start | bytes 663560 | tf_op jit(solution)/shard_map/ppermute | solution.py:453
  18.6 1.2 %copy-start.1 = (bf16[16,128,256]{2,1,0:T(8,128)(2,1)S(1)}, bf16[16,128,256]{2,1,0:T(8,128)(2,1)}, u32[]{:S(2)}) copy-start(bf16[16,128,256]{2,1,0:T(8,128)(2,1)} %cot_ref.3) | copy-start | bytes 3145732
  19.8 1.0 copy-start.4
  53.4 2.1 %collective-permute-start.4 = (bf16[64,8,640]{2,1,0:T(8,128)(2,1)S(1)}, bf16[64,8,640]{2,1,0:T(8,128)(2,1)S(1)}, u32[]{:S(2)}, u32[]{:S(2)}) collective-permute-start(bf16[64,8,640]{2,1,0:T(8,128)(2,1)S(1)} %get-tuple-element.26), channel_id=1, source_target_pairs={{0,8},{8,0},{1,9},{9,1},{2,10},{10,2},{3,11},{11,3},{4,12},{12,4},... | collective-permute-start | bytes 1966088 | tf_op jit(solution)/shard_map/ppermute | solution.py:520
  56.5 11.8 %collective-permute-start.6 = (bf16[16,8,256]{2,1,0:T(8,128)(2,1)S(1)}, bf16[16,8,256]{2,1,0:T(8,128)(2,1)S(1)}, u32[]{:S(2)}, u32[]{:S(2)}) collective-permute-start(bf16[16,8,256]{2,1,0:T(8,128)(2,1)S(1)} %get-tuple-element.44), channel_id=1, source_target_pairs={{8,16},{24,32},{40,48},{56,64},{72,80},{88,96},{104,112},{120,0},{... | collective-permute-start | bytes 196616 | tf_op jit(solution)/shard_map/ppermute | solution.py:432
  61.1 7.2 %collective-permute-start.5 = (bf16[16,8,256]{2,1,0:T(8,128)(2,1)S(1)}, bf16[16,8,256]{2,1,0:T(8,128)(2,1)S(1)}, u32[]{:S(2)}, u32[]{:S(2)}) collective-permute-start(bf16[16,8,256]{2,1,0:T(8,128)(2,1)S(1)} %get-tuple-element.45), channel_id=1, source_target_pairs={{0,8},{8,0},{1,9},{9,1},{2,10},{10,2},{3,11},{11,3},{4,12},{12,4},... | collective-permute-start | bytes 196616 | tf_op jit(solution)/shard_map/ppermute | solution.py:433
  61.2 22.0 %all-to-all-start = ((bf16[64,8,640]{2,1,0:T(8,128)(2,1)}), bf16[64,8,640]{2,1,0:T(8,128)(2,1)S(1)}, u32[]{:S(2)}, u32[]{:S(2)}) async-start(bf16[64,8,640]{2,1,0:T(8,128)(2,1)} %add_convert_fusion), calls=%async_computation | async-start | bytes 1310720 | tf_op jit(solution)/shard_map/all_to_all | solution.py:524
  69.0 15.4 %collective-permute-start.7 = (bf16[3,144,256]{2,1,0:T(8,128)(2,1)}, bf16[3,144,256]{2,1,0:T(8,128)(2,1)S(1)}, u32[]{:S(2)}, u32[]{:S(2)}) collective-permute-start(bf16[3,144,256]{2,1,0:T(8,128)(2,1)} %pad_maximum_fusion.2), channel_id=1, source_target_pairs={{0,1},{1,2},{2,3},{3,4},{4,5},{5,6},{6,7},{7,0},{8,9},{9,10},{10,1... | collective-permute-start | bytes 663560 | tf_op jit(solution)/shard_map/ppermute | solution.py:453
  71.3 13.2 %collective-permute-start.8 = (bf16[3,144,256]{2,1,0:T(8,128)(2,1)}, bf16[3,144,256]{2,1,0:T(8,128)(2,1)S(1)}, u32[]{:S(2)}, u32[]{:S(2)}) collective-permute-start(bf16[3,144,256]{2,1,0:T(8,128)(2,1)} %pad_maximum_fusion.3), channel_id=1, source_target_pairs={{0,7},{1,0},{2,1},{3,2},{4,3},{5,4},{6,5},{7,6},{8,15},{9,8},{10,9... | collective-permute-start | bytes 663560 | tf_op jit(solution)/shard_map/ppermute | solution.py:453
  83.3 9.5 %copy-start.2 = (bf16[16,128,256]{2,1,0:T(8,128)(2,1)S(1)}, bf16[16,128,256]{2,1,0:T(8,128)(2,1)}, u32[]{:S(2)}) copy-start(bf16[16,128,256]{2,1,0:T(8,128)(2,1)} %cot_ref.3) | copy-start | bytes 3145732
  85.3 22.0 %all-to-all-start.1 = ((bf16[64,8,640]{2,1,0:T(8,128)(2,1)}), bf16[64,8,640]{2,1,0:T(8,128)(2,1)S(1)}, u32[]{:S(2)}, u32[]{:S(2)}) async-start(bf16[64,8,640]{2,1,0:T(8,128)(2,1)} %broadcast_in_dim.2), calls=%async_computation.1 | async-start | bytes 1310720 | tf_op jit(solution)/shard_map/all_to_all | solution.py:535
  107.3 2.1 %collective-permute-start.9 = (bf16[64,8,640]{2,1,0:T(8,128)(2,1)S(1)}, bf16[64,8,640]{2,1,0:T(8,128)(2,1)S(1)}, u32[]{:S(2)}, u32[]{:S(2)}) collective-permute-start(bf16[64,8,640]{2,1,0:T(8,128)(2,1)S(1)} %all-to-all-done.1.mine_ref), channel_id=1, source_target_pairs={{0,8},{8,0},{1,9},{9,1},{2,10},{10,2},{3,11},{11,3},{4,12},{12,4},... | collective-permute-start | bytes 1966088 | tf_op jit(solution)/shard_map/ppermute | solution.py:551

commit v4 on v3

--- a/solution.py
+++ b/solution.py
@@ -16,7 +16,7 @@
 SPAN = 16
 EDGE = 8
 SLOTS = 64
-FORWARD_VMEM = 36 * 1024 * 1024
+FORWARD_VMEM = 51 * 1024 * 1024
 BACKWARD_VMEM = 28 * 1024 * 1024
 GROUP = 4
 CUTS = ((0, 2), (2, 4), (4, 7))
@@ -204,23 +204,23 @@
 
 
 def forward_kernel(
-    main_ref,
+    main_hbm,
     near_ref,
     far_ref,
     south_ref,
     north_ref,
-    cot_ref,
+    cot_hbm,
     sea_ref,
     slot_ref,
     taps_ref,
     gain_ref,
     bias_ref,
-    w_in_ref,
+    w_in_hbm,
     b_in_ref,
-    w_out_ref,
+    w_out_hbm,
     scale_ref,
-    out_ref,
-    gm_ref,
+    out_hbm,
+    gm_hbm,
     keep_ref,
     send_ref,
     wide,
@@ -236,19 +236,45 @@
     acc_in,
     acc_out,
     acc_scale,
+    main_ref,
+    cot_ref,
+    w_in_ref,
+    w_out_ref,
+    out_ref,
+    gm_ref,
+    sems,
 ):
+    moves = [
+        pltpu.make_async_copy(source, target, sems.at[n])
+        for n, (source, target) in enumerate(
+            (
+                (main_hbm, main_ref),
+                (cot_hbm, cot_ref),
+                (w_in_hbm, w_in_ref),
+                (w_out_hbm, w_out_ref),
+                (gm_ref, gm_hbm),
+                (out_ref, out_hbm),
+            )
+        )
+    ]
+    for move in moves[:4]:
+        move.start()
     rows = main_ref.shape[0]
     ff = w_in_ref.shape[1]
     width = 2 * HALF
     cells = 2 * STEP * SPAN
     build_weights(taps_ref, w_ref, False)
+    moves[0].wait()
     assemble(main_ref, near_ref, far_ref, south_ref, north_ref, wide, xs, xs_wide)
+    moves[1].wait()
     stage_cotangent(cot_ref, sea_ref, slot_ref, SLOTS, out_wide, mask_wide)
     acc_in[...] = jnp.zeros_like(acc_in)
     acc_out[...] = jnp.zeros_like(acc_out)
     acc_scale[...] = jnp.zeros_like(acc_scale)
     gain, bias, scale = gain_ref[...], bias_ref[...], scale_ref[...]
 
+    moves[2].wait()
+    moves[3].wait()
     acc_taps[...] = jnp.zeros_like(acc_taps)
     for h in range(2):
         gm_xs[h, 0:2] = jnp.zeros((2, STEP, SPAN, HALF), F32)
@@ -365,6 +391,8 @@
     lax.fori_loop(0, rows // 2, pair_step, 0)
 
     finish(rows // 2 - 1)
+    moves[4].start()
+    moves[5].start()
     for h in range(2):
         for i in range(KS):
             add_taps(gm_xs, xs_wide, acc_taps, h, i, rows // 2 - 1)
@@ -377,6 +405,9 @@
     @pl.when(core != 0)
     def _():
         pack_sums((send_ref, keep_ref), acc_in, acc_out, acc_scale, acc_taps)
+
+    moves[4].wait()
+    moves[5].wait()
 
 
 def backward_kernel(
@@ -462,6 +493,7 @@
     padded = rows + 2 * MARGIN
     ext = STEP + 2 * MARGIN
     vmem = pl.BlockSpec(memory_space=pltpu.VMEM)
+    hbm = pl.BlockSpec(memory_space=pl.ANY)
     wide = pltpu.VMEM((2, padded, tile + 2 * EDGE, HALF), F32)
     xs = pltpu.VMEM((2, padded, ext, SPAN, HALF), BF16)
     weights = pltpu.VMEM((2, TAPS * 256, 256), BF16)
@@ -477,8 +509,8 @@
             jax.ShapeDtypeStruct((chips, 8, chunk), BF16),
             jax.ShapeDtypeStruct((chips, 8, chunk), BF16),
         ),
-        in_specs=[vmem] * 15,
-        out_specs=(vmem,) * 4,
+        in_specs=[hbm] + [vmem] * 4 + [hbm] + [vmem] * 5 + [hbm, vmem, hbm, vmem],
+        out_specs=(hbm, hbm, vmem, vmem),
         scratch_shapes=[
             wide,
             xs,
@@ -493,6 +525,13 @@
             pltpu.VMEM((width, ff), F32),
             pltpu.VMEM((width, ff), F32),
             pltpu.VMEM((8, width), F32),
+            pltpu.VMEM(features.shape, BF16),
+            pltpu.VMEM(features.shape, BF16),
+            pltpu.VMEM(w_in.shape, BF16),
+            pltpu.VMEM(w_out.shape, BF16),
+            pltpu.VMEM(features.shape, BF16),
+            pltpu.VMEM(features.shape, BF16),
+            pltpu.SemaphoreType.DMA((6,)),
         ],
         compiler_params=pltpu.CompilerParams(vmem_limit_bytes=FORWARD_VMEM),
         cost_estimate=pl.CostEstimate(

time: 113 us -> 110 us (0.973)
  local copies, waits for them, and re-layouts: 4.35 us -> 2.09 us
    unnamed x25 -> x23, local copies, waits for them, and re-layouts: 2.39 us -> 0.13 us
where the time goes in v4:
time: 110 us; the launch traced here: 109 us
  Pallas kernels  45 us (41%)
  starting transfers between devices  33.7 us (31%)
  waiting for transfers between devices  23.4 us (21%)
  other arithmetic  3.55 us (3%)
  local copies, waits for them, and re-layouts  2.09 us (2%)
    pallas_call x1, Pallas kernels, on_device(): pl.pallas_call(forward_kernel, out_shape=(jax.ShapeDtypeStruct(features.s...  31.9 us
    pallas_call x1, Pallas kernels, on_device(): pl.pallas_call(backward_kernel, out_shape=jax.ShapeDtypeStruct(features.s...  11.3 us
    ppermute x2, starting transfers between devices, rim_sides(): far = lax.ppermute(jnp.where(even, low, high), LON, across)  10.3 us
    all_to_all x1, waiting for transfers between devices, on_device(): lax.all_to_all(sums, CHIPS, split_axis=0, concat_axis=0, tiled=True)  9.3 us
    ppermute x4, starting transfers between devices, rim_ends(): return (lax.ppermute(up, LAT, forward), lax.ppermute(down, LAT, backward))  8.5 us
    all_to_all x1, starting transfers between devices, on_device(): lax.all_to_all(jnp.broadcast_to(own[None], (chips,) + own.shape), CHIPS,...  7.66 us
    all_to_all x1, starting transfers between devices, on_device(): lax.all_to_all(sums, CHIPS, split_axis=0, concat_axis=0, tiled=True)  7.14 us
    ppermute x4, waiting for transfers between devices, rim_ends(): return (lax.ppermute(up, LAT, forward), lax.ppermute(down, LAT, backward))  5.83 us
  transfers between devices with their start and end apart: 12, of which 7 were waited for; matrix products, arithmetic and copies ran while one was open for 2% of the time, Pallas kernels for 10%

profile of v4, /device:TPU:0, one launch (start us, length us, event | category | flops | bytes accessed | tf_op | source)
XLA Modules:
  0.0 108.6 jit_solution(16630168411076122490)
XLA Ops:
  0.7 1.0 broadcast_select_fusion.2
  1.7 5.7 %collective-permute-start.1 = (bf16[16,8,256]{2,1,0:T(8,128)(2,1)S(1)}, bf16[16,8,256]{2,1,0:T(8,128)(2,1)S(1)}, u32[]{:S(2)}, u32[]{:S(2)}) collective-permute-start(bf16[16,8,256]{2,1,0:T(8,128)(2,1)S(1)} %get-tuple-element.48), channel_id=1, source_target_pairs={{8,16},{24,32},{40,48},{56,64},{72,80},{88,96},{104,112},{120,0},{... | collective-permute-start | bytes 196616 | tf_op jit(solution)/shard_map/ppermute | solution.py:463
  7.4 0.0 collective-permute-start
  7.4 1.0 fusion.1
  8.4 0.9 collective-permute-done.1.far_ref
  9.3 0.0 collective-permute-done.near_ref
  9.4 1.6 %collective-permute-start.2 = (bf16[3,144,256]{2,1,0:T(8,128)(2,1)S(1)}, bf16[3,144,256]{2,1,0:T(8,128)(2,1)S(1)}, u32[]{:S(2)}, u32[]{:S(2)}) collective-permute-start(bf16[3,144,256]{2,1,0:T(8,128)(2,1)S(1)} %pad_maximum_fusion), channel_id=1, source_target_pairs={{0,1},{1,2},{2,3},{3,4},{4,5},{5,6},{6,7},{7,0},{8,9},{9,10},{10,1... | collective-permute-start | bytes 663560 | tf_op jit(solution)/shard_map/ppermute | solution.py:484
  11.0 2.7 %collective-permute-start.3 = (bf16[3,144,256]{2,1,0:T(8,128)(2,1)S(1)}, bf16[3,144,256]{2,1,0:T(8,128)(2,1)S(1)}, u32[]{:S(2)}, u32[]{:S(2)}) collective-permute-start(bf16[3,144,256]{2,1,0:T(8,128)(2,1)S(1)} %pad_maximum_fusion.1), channel_id=1, source_target_pairs={{0,7},{1,0},{2,1},{3,2},{4,3},{5,4},{6,5},{7,6},{8,15},{9,8},{10,9... | collective-permute-start | bytes 663560 | tf_op jit(solution)/shard_map/ppermute | solution.py:484
  13.8 0.1 copy.17.slot_ref
  13.8 4.7 %collective-permute-done.2.south_ref = bf16[3,144,256]{2,1,0:T(8,128)(2,1)S(1)} collective-permute-done((bf16[3,144,256]{2,1,0:T(8,128)(2,1)S(1)}, bf16[3,144,256]{2,1,0:T(8,128)(2,1)S(1)}, u32[]{:S(2)}, u32[]{:S(2)}) %collective-permute-start.2) | collective-permute-done | bytes 221216 | tf_op jit(solution)/shard_map/ppermute | solution.py:484
  18.5 0.0 collective-permute-done.3.north_ref
  18.6 31.9 %forward.1 = (bf16[16,128,256]{2,1,0:T(8,128)(2,1)}, bf16[16,128,256]{2,1,0:T(8,128)(2,1)}, bf16[64,8,640]{2,1,0:T(8,128)(2,1)S(1)}, bf16[64,8,640]{2,1,0:T(8,128)(2,1)S(1)}) custom-call(bf16[16,128,256]{2,1,0:T(8,128)(2,1)} %main_hbm.1, bf16[16,8,256]{2,1,0:T(8,128)(2,1)S(1)} %collective-permute-done.near_ref, ...), custom_call_target="tpu_custom_call" | custom-call | flops 14000000000 | bytes 8000000 | tf_op jit(solution)/shard_map/forward/pallas_call | solution.py:504
  50.5 0.0 copy-start
  50.5 0.1 collective-permute-start.4
  50.6 2.1 %collective-permute-done.4 = bf16[64,8,640]{2,1,0:T(8,128)(2,1)S(1)} collective-permute-done((bf16[64,8,640]{2,1,0:T(8,128)(2,1)S(1)}, bf16[64,8,640]{2,1,0:T(8,128)(2,1)S(1)}, u32[]{:S(2)}, u32[]{:S(2)}) %collective-permute-start.4) | collective-permute-done | bytes 655392 | tf_op jit(solution)/shard_map/ppermute | solution.py:559
  52.7 1.0 add_convert_fusion
  53.7 4.6 %collective-permute-start.6 = (bf16[16,8,256]{2,1,0:T(8,128)(2,1)S(1)}, bf16[16,8,256]{2,1,0:T(8,128)(2,1)S(1)}, u32[]{:S(2)}, u32[]{:S(2)}) collective-permute-start(bf16[16,8,256]{2,1,0:T(8,128)(2,1)S(1)} %get-tuple-element.44), channel_id=1, source_target_pairs={{8,16},{24,32},{40,48},{56,64},{72,80},{88,96},{104,112},{120,0},{... | collective-permute-start | bytes 196616 | tf_op jit(solution)/shard_map/ppermute | solution.py:463
  58.4 7.1 %all-to-all-start = ((bf16[64,8,640]{2,1,0:T(8,128)(2,1)}), bf16[64,8,640]{2,1,0:T(8,128)(2,1)S(1)}, u32[]{:S(2)}, u32[]{:S(2)}) async-start(bf16[64,8,640]{2,1,0:T(8,128)(2,1)} %add_convert_fusion), calls=%async_computation | async-start | bytes 1310720 | tf_op jit(solution)/shard_map/all_to_all | solution.py:563
  65.6 0.0 collective-permute-done.6.far_ref
  65.6 0.7 pad_maximum_fusion.2
  66.3 1.6 %collective-permute-start.7 = (bf16[3,144,256]{2,1,0:T(8,128)(2,1)}, bf16[3,144,256]{2,1,0:T(8,128)(2,1)S(1)}, u32[]{:S(2)}, u32[]{:S(2)}) collective-permute-start(bf16[3,144,256]{2,1,0:T(8,128)(2,1)} %pad_maximum_fusion.2), channel_id=1, source_target_pairs={{0,1},{1,2},{2,3},{3,4},{4,5},{5,6},{6,7},{7,0},{8,9},{9,10},{10,1... | collective-permute-start | bytes 663560 | tf_op jit(solution)/shard_map/ppermute | solution.py:484
  67.9 0.7 pad_maximum_fusion.3
  68.6 2.6 %collective-permute-start.8 = (bf16[3,144,256]{2,1,0:T(8,128)(2,1)}, bf16[3,144,256]{2,1,0:T(8,128)(2,1)S(1)}, u32[]{:S(2)}, u32[]{:S(2)}) collective-permute-start(bf16[3,144,256]{2,1,0:T(8,128)(2,1)} %pad_maximum_fusion.3), channel_id=1, source_target_pairs={{0,7},{1,0},{2,1},{3,2},{4,3},{5,4},{6,5},{7,6},{8,15},{9,8},{10,9... | collective-permute-start | bytes 663560 | tf_op jit(solution)/shard_map/ppermute | solution.py:484
  71.1 9.3 %all-to-all-done = bf16[64,8,640]{2,1,0:T(8,128)(2,1)S(1)} async-done(((bf16[64,8,640]{2,1,0:T(8,128)(2,1)}), bf16[64,8,640]{2,1,0:T(8,128)(2,1)S(1)}, u32[]{:S(2)}, u32[]{:S(2)}) %all-to-all-start) | async-done | bytes 655392 | tf_op jit(solution)/shard_map/all_to_all | solution.py:563
  80.4 0.1 reduce_sum.12
  80.6 1.2 %collective-permute-done.7.south_ref = bf16[3,144,256]{2,1,0:T(8,128)(2,1)S(1)} collective-permute-done((bf16[3,144,256]{2,1,0:T(8,128)(2,1)}, bf16[3,144,256]{2,1,0:T(8,128)(2,1)S(1)}, u32[]{:S(2)}, u32[]{:S(2)}) %collective-permute-start.7) | collective-permute-done | bytes 221216 | tf_op jit(solution)/shard_map/ppermute | solution.py:484
  81.7 0.9 broadcast_in_dim.2
  82.6 7.7 %all-to-all-start.1 = ((bf16[64,8,640]{2,1,0:T(8,128)(2,1)}), bf16[64,8,640]{2,1,0:T(8,128)(2,1)S(1)}, u32[]{:S(2)}, u32[]{:S(2)}) async-start(bf16[64,8,640]{2,1,0:T(8,128)(2,1)} %broadcast_in_dim.2), calls=%async_computation.1 | async-start | bytes 1310720 | tf_op jit(solution)/shard_map/all_to_all | solution.py:574
  90.3 11.3 %backward.1 = bf16[16,128,256]{2,1,0:T(8,128)(2,1)} custom-call(bf16[16,128,256]{2,1,0:T(8,128)(2,1)S(1)} %copy-done, bf16[16,8,256]{2,1,0:T(8,128)(2,1)S(1)} %collective-permute-done.5.near_ref, bf16[16,8,256]{2,1,0:T(8,128)(2,1)S(1)} %collective-permute-done.6.far_ref, bf16[3,144,256]{2,1,0:T(8,128)(2,1)S(1)} %collective-permute-done.7.south_ref, ...), custom_call_target="tpu_custom_call" | custom-call | flops 7000000000 | bytes 4000000 | tf_op jit(solution)/shard_map/backward/pallas_call | solution.py:577
  101.6 3.2 %all-to-all-done.1.mine_ref = bf16[64,8,640]{2,1,0:T(8,128)(2,1)S(1)} async-done(((bf16[64,8,640]{2,1,0:T(8,128)(2,1)}), bf16[64,8,640]{2,1,0:T(8,128)(2,1)S(1)}, u32[]{:S(2)}, u32[]{:S(2)}) %all-to-all-start.1) | async-done | bytes 655392 | tf_op jit(solution)/shard_map/all_to_all | solution.py:574
  104.8 2.1 %collective-permute-done.9.other_ref = bf16[64,8,640]{2,1,0:T(8,128)(2,1)S(1)} collective-permute-done((bf16[64,8,640]{2,1,0:T(8,128)(2,1)S(1)}, bf16[64,8,640]{2,1,0:T(8,128)(2,1)S(1)}, u32[]{:S(2)}, u32[]{:S(2)}) %collective-permute-start.9) | collective-permute-done | bytes 655392 | tf_op jit(solution)/shard_map/ppermute | solution.py:590
  106.9 1.8 %unpack.1 = (f32[256,1024]{1,0:T(8,128)}, f32[1024,256]{1,0:T(8,128)}, f32[7,7,256]{2,1,0:T(8,128)}, f32[1,256]{1,0:T(1,128)}) custom-call(bf16[64,8,640]{2,1,0:T(8,128)(2,1)S(1)} %all-to-all-done.1.mine_ref, bf16[64,8,640]{2,1,0:T(8,128)(2,1)S(1)} %collective-permute-done.9.other_ref), custom_call_target="tpu_custom_call" | custom-call | tf_op jit(solution)/shard_map/unpack/pallas_call | solution.py:592
  (31 shorter events, 0.1 us)
Async XLA Ops:
  0.6 13.1 %copy-start.10 = (s32[16,1]{0,1:T(1,128)S(1)}, s32[16,1]{0,1:T(1,128)}, u32[]{:S(2)}) copy-start(s32[16,1]{0,1:T(1,128)} %param.14) | copy-start | bytes 196
  0.6 17.9 %copy-start.4 = (f32[7,7,256]{2,1,0:T(8,128)S(1)}, f32[7,7,256]{2,1,0:T(8,128)}, u32[]{:S(2)}) copy-start(f32[7,7,256]{2,1,0:T(8,128)} %taps_ref.3) | copy-start | bytes 150532
  0.7 17.9 %copy-start.9 = (f32[256]{0:T(256)S(1)}, f32[256]{0:T(256)}, u32[]{:S(2)}) copy-start(f32[256]{0:T(256)} %param.21) | copy-start | bytes 3076
  0.7 17.9 %copy-start.3 = (bf16[1024,256]{1,0:T(8,128)(2,1)S(1)}, bf16[1024,256]{1,0:T(8,128)(2,1)}, u32[]{:S(2)}) copy-start(bf16[1024,256]{1,0:T(8,128)(2,1)} %w_out_hbm.1) | copy-start | bytes 1572868
  0.7 17.9 %copy-start.6 = (f32[1024]{0:T(1024)S(1)}, f32[1024]{0:T(1024)}, u32[]{:S(2)}) copy-start(f32[1024]{0:T(1024)} %param.19) | copy-start | bytes 12292
  0.7 17.9 %copy-start.2 = (bf16[256,1024]{1,0:T(8,128)(2,1)S(1)}, bf16[256,1024]{1,0:T(8,128)(2,1)}, u32[]{:S(2)}) copy-start(bf16[256,1024]{1,0:T(8,128)(2,1)} %w_in_hbm.1) | copy-start | bytes 1572868
  0.7 17.9 %copy-start.8 = (f32[256]{0:T(256)S(1)}, f32[256]{0:T(256)}, u32[]{:S(2)}) copy-start(f32[256]{0:T(256)} %param.17) | copy-start | bytes 3076
  0.7 17.9 %copy-start.7 = (f32[256]{0:T(256)S(1)}, f32[256]{0:T(256)}, u32[]{:S(2)}) copy-start(f32[256]{0:T(256)} %param.16) | copy-start | bytes 3076
  0.7 17.9 %copy-start.5 = (s32[16,128]{1,0:T(8,128)S(1)}, s32[16,128]{1,0:T(8,128)}, u32[]{:S(2)}) copy-start(s32[16,128]{1,0:T(8,128)} %sea_ref.1) | copy-start | bytes 24580
  1.7 7.6 %collective-permute-start.1 = (bf16[16,8,256]{2,1,0:T(8,128)(2,1)S(1)}, bf16[16,8,256]{2,1,0:T(8,128)(2,1)S(1)}, u32[]{:S(2)}, u32[]{:S(2)}) collective-permute-start(bf16[16,8,256]{2,1,0:T(8,128)(2,1)S(1)} %get-tuple-element.48), channel_id=1, source_target_pairs={{8,16},{24,32},{40,48},{56,64},{72,80},{88,96},{104,112},{120,0},{... | collective-permute-start | bytes 196616 | tf_op jit(solution)/shard_map/ppermute | solution.py:463
  7.4 2.0 %collective-permute-start = (bf16[16,8,256]{2,1,0:T(8,128)(2,1)S(1)}, bf16[16,8,256]{2,1,0:T(8,128)(2,1)S(1)}, u32[]{:S(2)}, u32[]{:S(2)}) collective-permute-start(bf16[16,8,256]{2,1,0:T(8,128)(2,1)S(1)} %get-tuple-element.49), channel_id=1, source_target_pairs={{0,8},{8,0},{1,9},{9,1},{2,10},{10,2},{3,11},{11,3},{4,12},{12,4},... | collective-permute-start | bytes 196616 | tf_op jit(solution)/shard_map/ppermute | solution.py:464
  9.4 9.1 %collective-permute-start.2 = (bf16[3,144,256]{2,1,0:T(8,128)(2,1)S(1)}, bf16[3,144,256]{2,1,0:T(8,128)(2,1)S(1)}, u32[]{:S(2)}, u32[]{:S(2)}) collective-permute-start(bf16[3,144,256]{2,1,0:T(8,128)(2,1)S(1)} %pad_maximum_fusion), channel_id=1, source_target_pairs={{0,1},{1,2},{2,3},{3,4},{4,5},{5,6},{6,7},{7,0},{8,9},{9,10},{10,1... | collective-permute-start | bytes 663560 | tf_op jit(solution)/shard_map/ppermute | solution.py:484
  11.0 7.5 %collective-permute-start.3 = (bf16[3,144,256]{2,1,0:T(8,128)(2,1)S(1)}, bf16[3,144,256]{2,1,0:T(8,128)(2,1)S(1)}, u32[]{:S(2)}, u32[]{:S(2)}) collective-permute-start(bf16[3,144,256]{2,1,0:T(8,128)(2,1)S(1)} %pad_maximum_fusion.1), channel_id=1, source_target_pairs={{0,7},{1,0},{2,1},{3,2},{4,3},{5,4},{6,5},{7,6},{8,15},{9,8},{10,9... | collective-permute-start | bytes 663560 | tf_op jit(solution)/shard_map/ppermute | solution.py:484
  50.5 3.2 %copy-start = (bf16[16,128,256]{2,1,0:T(8,128)(2,1)S(1)}, bf16[16,128,256]{2,1,0:T(8,128)(2,1)}, u32[]{:S(2)}) copy-start(bf16[16,128,256]{2,1,0:T(8,128)(2,1)} %get-tuple-element.31.main_ref) | copy-start | bytes 3145732
  50.5 2.2 %collective-permute-start.4 = (bf16[64,8,640]{2,1,0:T(8,128)(2,1)S(1)}, bf16[64,8,640]{2,1,0:T(8,128)(2,1)S(1)}, u32[]{:S(2)}, u32[]{:S(2)}) collective-permute-start(bf16[64,8,640]{2,1,0:T(8,128)(2,1)S(1)} %get-tuple-element.26), channel_id=1, source_target_pairs={{0,8},{8,0},{1,9},{9,1},{2,10},{10,2},{3,11},{11,3},{4,12},{12,4},... | collective-permute-start | bytes 1966088 | tf_op jit(solution)/shard_map/ppermute | solution.py:559
  53.7 11.8 %collective-permute-start.6 = (bf16[16,8,256]{2,1,0:T(8,128)(2,1)S(1)}, bf16[16,8,256]{2,1,0:T(8,128)(2,1)S(1)}, u32[]{:S(2)}, u32[]{:S(2)}) collective-permute-start(bf16[16,8,256]{2,1,0:T(8,128)(2,1)S(1)} %get-tuple-element.44), channel_id=1, source_target_pairs={{8,16},{24,32},{40,48},{56,64},{72,80},{88,96},{104,112},{120,0},{... | collective-permute-start | bytes 196616 | tf_op jit(solution)/shard_map/ppermute | solution.py:463
  58.4 7.2 %collective-permute-start.5 = (bf16[16,8,256]{2,1,0:T(8,128)(2,1)S(1)}, bf16[16,8,256]{2,1,0:T(8,128)(2,1)S(1)}, u32[]{:S(2)}, u32[]{:S(2)}) collective-permute-start(bf16[16,8,256]{2,1,0:T(8,128)(2,1)S(1)} %get-tuple-element.45), channel_id=1, source_target_pairs={{0,8},{8,0},{1,9},{9,1},{2,10},{10,2},{3,11},{11,3},{4,12},{12,4},... | collective-permute-start | bytes 196616 | tf_op jit(solution)/shard_map/ppermute | solution.py:464
  58.4 22.0 %all-to-all-start = ((bf16[64,8,640]{2,1,0:T(8,128)(2,1)}), bf16[64,8,640]{2,1,0:T(8,128)(2,1)S(1)}, u32[]{:S(2)}, u32[]{:S(2)}) async-start(bf16[64,8,640]{2,1,0:T(8,128)(2,1)} %add_convert_fusion), calls=%async_computation | async-start | bytes 1310720 | tf_op jit(solution)/shard_map/all_to_all | solution.py:563
  66.3 15.4 %collective-permute-start.7 = (bf16[3,144,256]{2,1,0:T(8,128)(2,1)}, bf16[3,144,256]{2,1,0:T(8,128)(2,1)S(1)}, u32[]{:S(2)}, u32[]{:S(2)}) collective-permute-start(bf16[3,144,256]{2,1,0:T(8,128)(2,1)} %pad_maximum_fusion.2), channel_id=1, source_target_pairs={{0,1},{1,2},{2,3},{3,4},{4,5},{5,6},{6,7},{7,0},{8,9},{9,10},{10,1... | collective-permute-start | bytes 663560 | tf_op jit(solution)/shard_map/ppermute | solution.py:484
  68.6 13.2 %collective-permute-start.8 = (bf16[3,144,256]{2,1,0:T(8,128)(2,1)}, bf16[3,144,256]{2,1,0:T(8,128)(2,1)S(1)}, u32[]{:S(2)}, u32[]{:S(2)}) collective-permute-start(bf16[3,144,256]{2,1,0:T(8,128)(2,1)} %pad_maximum_fusion.3), channel_id=1, source_target_pairs={{0,7},{1,0},{2,1},{3,2},{4,3},{5,4},{6,5},{7,6},{8,15},{9,8},{10,9... | collective-permute-start | bytes 663560 | tf_op jit(solution)/shard_map/ppermute | solution.py:484
  80.6 9.7 %copy-start.1 = (bf16[16,128,256]{2,1,0:T(8,128)(2,1)S(1)}, bf16[16,128,256]{2,1,0:T(8,128)(2,1)}, u32[]{:S(2)}) copy-start(bf16[16,128,256]{2,1,0:T(8,128)(2,1)} %cot_ref.1) | copy-start | bytes 3145732
  82.6 22.1 %all-to-all-start.1 = ((bf16[64,8,640]{2,1,0:T(8,128)(2,1)}), bf16[64,8,640]{2,1,0:T(8,128)(2,1)S(1)}, u32[]{:S(2)}, u32[]{:S(2)}) async-start(bf16[64,8,640]{2,1,0:T(8,128)(2,1)} %broadcast_in_dim.2), calls=%async_computation.1 | async-start | bytes 1310720 | tf_op jit(solution)/shard_map/all_to_all | solution.py:574
  104.8 2.1 %collective-permute-start.9 = (bf16[64,8,640]{2,1,0:T(8,128)(2,1)S(1)}, bf16[64,8,640]{2,1,0:T(8,128)(2,1)S(1)}, u32[]{:S(2)}, u32[]{:S(2)}) collective-permute-start(bf16[64,8,640]{2,1,0:T(8,128)(2,1)S(1)} %all-to-all-done.1.mine_ref), channel_id=1, source_target_pairs={{0,8},{8,0},{1,9},{9,1},{2,10},{10,2},{3,11},{11,3},{4,12},{12,4},... | collective-permute-start | bytes 1966088 | tf_op jit(solution)/shard_map/ppermute | solution.py:590
